TPU v7x, 32 devices: a whole 2x2x4 slice. The times are simulated.
32 devices in a mesh: az: 8 (over z, x), rg: 4 (over y, core).
Axes of the slice: x: 2, y: 2, z: 4, core: 2. Of those that a mesh axis runs over, the one named last changes fastest.
Arguments:
- raw_echo: bfloat16 [2, 8192, 1536], P(None, 'az', 'rg'), may hold values from -6 to 6
- range_chirp: bfloat16 [2, 512], replicated, may hold values from -0.1875 to 0.1875
- migration_taps: bfloat16 [8, 1536], P(None, 'rg'), may hold values from -2.09375 to 2.09375
- block_shift: int32 [12], P('rg'), may hold values from -60 to 60, as said below
- azimuth_chirp: bfloat16 [12, 2, 512], P('rg'), may hold values from -0.1875 to 0.1875
Outputs:
- focused_image: float32 [2, 8192, 1536], P(None, 'az', 'rg')
Inputs may be any that keep to these rules, and one draw needn't show every extreme that they name: `block_shift`: every range block of 128 cells has one shift; the values -60 and 60 both occur in every draw.
All inputs are finite; a program needn't handle non-finite values.
Results may differ from a plain program's by a relative error of at most 0.0041.
Values may be sent and summed in bfloat16 or wider, within the bound.
No kernel may reach another device: no remote copies, remote signals or barrier semaphores. Data moves between devices by JAX's collectives and lax.ppermute only.
A program may use at most 64 MiB of HBM per device.

v0:
```python
import functools

import jax
import jax.numpy as jnp
from jax import lax
from jax.experimental import pallas as pl
from jax.experimental.pallas import tpu as pltpu
from jax.sharding import PartitionSpec as P

MAXS = 60
LANES = 128
HALF = 64
CHUNK = 256
PAD = 16
VMEM_LIMIT = 20 * 1024 * 1024
F32 = jnp.float32
BF16 = jnp.bfloat16


def params():
    return pltpu.CompilerParams(vmem_limit_bytes=VMEM_LIMIT)


def whole(shape):
    return pl.BlockSpec(shape, lambda *_: (0,) * len(shape))


def in_hbm(x):
    return pltpu.with_memory_space_constraint(x, pltpu.HBM)


def lane_roll(x):
    return pltpu.roll(x, HALF, 1)


def low_lanes(rows):
    return lax.broadcasted_iota(jnp.int16, (rows, LANES), 1) < HALF


def swap_pairs(count, first):
    pairs = []
    for i in range(first, count - 1, 2):
        pairs += [(i, i + 1), (i + 1, i)]
    return pairs


def swap(x, axis, first):
    return lax.ppermute(x, axis, swap_pairs(lax.axis_size(axis), first))


def by_parity(axis, body):
    odd = lax.rem(lax.axis_index(axis), 2)
    pl.when(odd == 0)(lambda: body(0))
    pl.when(odd == 1)(lambda: body(1))


def shifted_rows(row, lead, width):
    taps = row.shape[1]
    padded = jnp.concatenate([row, jnp.zeros((1, width - taps), F32)], axis=1)
    return pltpu.roll(
        jnp.broadcast_to(padded, (LANES, width)), lead, 1, stride=1, stride_axis=0
    )


def range_toeplitz(range_ref, w_ref):
    depth = w_ref.shape[0] // 2
    real = shifted_rows(range_ref[0:1, :].astype(F32), 0, depth)
    imag = shifted_rows(range_ref[1:2, :].astype(F32), 0, depth)
    real_t, imag_t = real.T.astype(BF16), imag.T.astype(BF16)
    w_ref[0:depth, 0:LANES] = real_t
    w_ref[0:depth, LANES:] = -imag_t
    w_ref[depth:, 0:LANES] = imag_t
    w_ref[depth:, LANES:] = real_t


def migration_bands(taps_ref, shift_ref, m_ref):
    span = m_ref.shape[1]
    blocks = m_ref.shape[0]
    cells = taps_ref.shape[1]
    tap_count = taps_ref.shape[0]
    first = lax.axis_index("rg") * cells - HALF
    total = lax.axis_size("rg") * cells
    for b in range(blocks):
        source = lax.broadcasted_iota(jnp.int32, (span, LANES), 0)
        column = lax.broadcasted_iota(jnp.int32, (span, LANES), 1)
        tap = source - column - (HALF - tap_count // 2) - shift_ref[b][:1, :]
        place = source + first + b * LANES
        tap = jnp.where((place >= 0) & (place < total), tap, -1)
        matrix = jnp.zeros((span, LANES), F32)
        for k in range(tap_count):
            row = taps_ref[k : k + 1, b * LANES : (b + 1) * LANES].astype(F32)
            matrix = jnp.where(tap == k, row, matrix)
        m_ref[b] = matrix.astype(BF16)


def azimuth_weights_kernel(azimuth_ref, a_ref):
    steps, blocks, depth = a_ref.shape[0], a_ref.shape[1], a_ref.shape[3]
    gap = jnp.zeros((LANES, LANES), BF16)
    for b in range(blocks):
        for part in range(2):
            row = azimuth_ref[b, part : part + 1, :].astype(F32)
            rows = shifted_rows(row, 0, steps * depth - LANES).astype(BF16)
            upper = jnp.concatenate([rows, gap], axis=1)
            lower = jnp.concatenate([gap, rows], axis=1)
            base = part * CHUNK
            for k in range(steps):
                a_ref[k, b, base : base + LANES] = upper[:, k * depth : (k + 1) * depth]
                a_ref[k, b, base + LANES : base + CHUNK] = lower[:, k * depth : (k + 1) * depth]


def azimuth_weights(azimuth_chirp):
    blocks = azimuth_chirp.shape[0]
    steps = (azimuth_chirp.shape[2] + CHUNK) // CHUNK
    return pl.pallas_call(
        azimuth_weights_kernel,
        out_shape=jax.ShapeDtypeStruct((steps, blocks, 2 * CHUNK, CHUNK), BF16),
        in_specs=[pl.BlockSpec(memory_space=pltpu.VMEM)],
        out_specs=pl.BlockSpec(memory_space=pltpu.VMEM),
        compiler_params=params(),
        name="azimuth_weights",
    )(azimuth_chirp)


def tile_of(t):
    return slice(t * LANES, (t + 1) * LANES)


def edge_chunk(x_ref, s_ref, start, targets):
    picked = pl.ds(start, CHUNK)
    half = CHUNK // 2
    low, low_half = low_lanes(CHUNK), low_lanes(half)
    count = x_ref.shape[2] // LANES
    for part in range(2):
        cells = [x_ref[part, picked, tile_of(t)] for t in range(count)]
        rolled = [lane_roll(c) for c in cells]
        tiles = [rolled[0]]
        tiles += [jnp.where(low, rolled[t], rolled[t + 1]) for t in range(count - 1)]
        tiles += [rolled[-1]]
        for t, tile in enumerate(tiles):
            s_ref[part, picked, tile_of(t)] = tile
        for out_ref, chunk, side in targets:
            inner = (1, 2) if side == 0 else (count - 2, count - 1)
            for i, t in enumerate(inner):
                at = (2 * part + i) * CHUNK
                out_ref[chunk, at : at + CHUNK, :] = tiles[t]
            at = 4 * CHUNK + part * half
            if side == 0:
                packed = jnp.where(low_half, cells[0][:half], rolled[0][half:])
            else:
                packed = jnp.where(low_half, rolled[-1][:half], cells[-1][half:])
            out_ref[chunk, at : at + half, :] = packed


def near_away_rows(rows):
    odd = lax.rem(lax.axis_index("az"), 2)
    last = rows - CHUNK
    near = pl.multiple_of((1 - odd) * last, CHUNK)
    away = pl.multiple_of(odd * last, CHUNK)
    return near, away


def edges_kernel(
    x_hbm, range_hbm, taps_hbm, shift_hbm, azimuth_hbm,
    s_ref, far_outer_ref, far_mid_ref, core_outer_ref, core_mid_ref,
    w_ref, taps_ref, splat_ref, azimuth_ref, x_ref, range_ref, shift_ref, sems,
):
    rows = x_ref.shape[1]
    near, away = near_away_rows(rows)
    starts = [near, away] + list(range(CHUNK, rows - CHUNK, CHUNK))
    moves = [
        (range_hbm, range_ref),
        (taps_hbm, taps_ref),
        (shift_hbm, shift_ref),
        (azimuth_hbm, azimuth_ref),
    ]
    small = len(moves)
    for start in starts:
        for part in range(2):
            picked = pl.ds(start, CHUNK)
            moves.append((x_hbm.at[part, picked, :], x_ref.at[part, picked, :]))
    copies = [
        pltpu.make_async_copy(source, target, sems.at[i])
        for i, (source, target) in enumerate(moves)
    ]
    for copy in copies:
        copy.start()
    for copy in copies[:small]:
        copy.wait()
    for ref in (core_outer_ref, core_mid_ref):
        extra = ref.shape[1] - 5 * CHUNK
        ref[:, 5 * CHUNK :, :] = jnp.zeros((ref.shape[0], extra, LANES), BF16)
    range_toeplitz(range_ref, w_ref)
    for b in range(splat_ref.shape[0]):
        splat_ref[b] = jnp.full(splat_ref.shape[1:], shift_ref[b], jnp.int32)

    def body(odd):
        for i, start in enumerate(starts):
            copies[small + 2 * i].wait()
            copies[small + 2 * i + 1].wait()
            outer = (core_outer_ref, far_outer_ref, i)
            core_ref, far_ref, chunk = outer if i < 2 else (core_mid_ref, far_mid_ref, i - 2)
            edge_chunk(x_ref, s_ref, start, [(core_ref, chunk, 1 - odd), (far_ref, chunk, odd)])

    by_parity("rg", body)


def range_edges(raw, range_chirp, migration_taps, block_shift, azimuth_chirp):
    chunks = raw.shape[1] // CHUNK
    blocks = block_shift.shape[0]
    depth = range_chirp.shape[1] + LANES
    args = (raw, range_chirp, migration_taps, block_shift, azimuth_chirp)
    return pl.pallas_call(
        edges_kernel,
        out_shape=(jax.ShapeDtypeStruct(raw.shape[:2] + (raw.shape[2] + LANES,), BF16),)
        + tuple(
            jax.ShapeDtypeStruct((n, 5 * CHUNK + extra, LANES), BF16)
            for n, extra in ((2, 0), (chunks - 2, 0), (2, 2 * PAD), (chunks - 2, PAD))
        )
        + (
            jax.ShapeDtypeStruct((2 * depth, 2 * LANES), BF16),
            jax.ShapeDtypeStruct(migration_taps.shape, BF16),
            jax.ShapeDtypeStruct((blocks, 8, LANES), jnp.int32),
            jax.ShapeDtypeStruct(azimuth_chirp.shape, BF16),
        ),
        in_specs=[pl.BlockSpec(memory_space=pltpu.HBM)] * len(args),
        out_specs=(pl.BlockSpec(memory_space=pltpu.VMEM),) * 9,
        scratch_shapes=[
            pltpu.VMEM(raw.shape, BF16),
            pltpu.VMEM(range_chirp.shape, BF16),
            pltpu.SMEM(block_shift.shape, jnp.int32),
            pltpu.SemaphoreType.DMA((2 * chunks + len(args) - 1,)),
        ],
        compiler_params=params(),
        name="range_edges",
    )(*(in_hbm(x) for x in args))


def window_tiles(s_ref, start, left, right, part):
    half = CHUNK // 2
    low = low_lanes(CHUNK)
    picked = pl.ds(start, CHUNK)
    last = s_ref.shape[2] // LANES - 1
    inner = slice(4 * CHUNK + part * half, 4 * CHUNK + (part + 1) * half)

    def full(halo):
        ref, chunk = halo
        return [
            ref[chunk, (2 * part + i) * CHUNK : (2 * part + i + 1) * CHUNK, :] for i in range(2)
        ]

    packed = left[0][left[1], inner, :]
    halo = jnp.concatenate([packed, lane_roll(packed)], axis=0)
    first = jnp.where(low, halo, s_ref[part, picked, tile_of(0)])
    packed = right[0][right[1], inner, :]
    halo = jnp.concatenate([lane_roll(packed), packed], axis=0)
    final = jnp.where(low, s_ref[part, picked, tile_of(last)], halo)
    own = [s_ref[part, picked, tile_of(t)] for t in range(1, last)]
    return full(left) + [first] + own + [final] + full(right)


def compress_chunk(s_ref, start, left, right, w_ref, m_ref, out_ref, out_start, c_ref):
    rows = CHUNK
    taps = w_ref.shape[0] // (2 * LANES)
    tiles = [window_tiles(s_ref, start, left, right, part) for part in range(2)]
    for j in range(c_ref.shape[1] // LANES):
        window = jnp.concatenate(tiles[0][j : j + taps] + tiles[1][j : j + taps], axis=1)
        result = jnp.dot(window, w_ref[...], preferred_element_type=F32).astype(BF16)
        c_ref[0:rows, tile_of(j)] = result[:, :LANES]
        c_ref[rows:, tile_of(j)] = result[:, LANES:]
    for b in range(m_ref.shape[0]):
        window = c_ref[:, b * LANES : b * LANES + 2 * LANES]
        result = jnp.dot(window, m_ref[b], preferred_element_type=F32).astype(BF16)
        out_ref[0, out_start : out_start + rows, tile_of(b)] = result[:rows]
        out_ref[1, out_start : out_start + rows, tile_of(b)] = result[rows:]


def compress_kernel(which, s_ref, core_ref, far_ref, w_ref, *refs):
    near, away = near_away_rows(s_ref.shape[1])
    if which == "near":
        taps_ref, splat_ref, out_ref, m_ref, *c_refs = refs
        jobs = [(near, 0)]
    else:
        m_ref, out_ref, *c_refs = refs
        jobs = [(CHUNK * (i + 1), i) for i in range(out_ref.shape[1] // CHUNK)]
        if which == "away":
            jobs = [(away, 1)]

    def body(odd):
        if which == "near":
            migration_bands(taps_ref, splat_ref, m_ref)
        for i, (start, chunk) in enumerate(jobs):
            core, far = (core_ref, chunk), (far_ref, chunk)
            left, right = (core, far) if odd else (far, core)
            compress_chunk(
                s_ref, start, left, right, w_ref, m_ref, out_ref, i * CHUNK, c_refs[i]
            )

    by_parity("rg", body)


def compress(which, shifted, core, far, w, *bands):
    rows, cells = shifted.shape[1], shifted.shape[2] - LANES
    count = rows // CHUNK - 2 if which == "mid" else 1
    args = (shifted, core, far, w) + bands
    out = (jax.ShapeDtypeStruct((2, count * CHUNK, cells), BF16),)
    if which == "near":
        out += (jax.ShapeDtypeStruct((cells // LANES, 2 * LANES, LANES), BF16),)
    result = pl.pallas_call(
        functools.partial(compress_kernel, which),
        out_shape=out,
        in_specs=[pl.BlockSpec(memory_space=pltpu.VMEM)] * len(args),
        out_specs=(pl.BlockSpec(memory_space=pltpu.VMEM),) * len(out),
        scratch_shapes=[pltpu.VMEM((2 * CHUNK, cells + LANES), BF16)] * count,
        compiler_params=params(),
        name="compress_" + which,
    )(*args)
    return result if which == "near" else result[0]


def lines(ref, chunk):
    return lambda part, lanes: ref[part, chunk * CHUNK : (chunk + 1) * CHUNK, lanes]


def correlate_block(a_ref, b, pairs):
    taps = [a_ref[k, b] for k, _ in pairs]
    windows = [
        jnp.concatenate([window(0, tile_of(b)), window(1, tile_of(b))], axis=1)
        for _, window in pairs
    ]
    result = jnp.dot(
        jnp.concatenate(taps, axis=1),
        jnp.concatenate(windows, axis=0),
        preferred_element_type=F32,
    )
    top, bottom = result[:CHUNK], result[CHUNK:]
    return top[:, :LANES] + bottom[:, LANES:], top[:, LANES:] - bottom[:, :LANES]


def focus_outer_kernel(a_ref, near_ref, away_ref, part_ref, mid_part_ref):
    mids, steps, blocks = mid_part_ref.shape[0], a_ref.shape[0], a_ref.shape[1]

    def body(odd):
        first, final = (near_ref, away_ref) if odd else (away_ref, near_ref)
        order = {0: lines(first, 0), mids + 1: lines(final, 0)}
        jobs = [(part_ref.at[0], 0), (part_ref.at[1], mids + 1)]
        jobs += [(mid_part_ref.at[i], i + 1) for i in range(mids)]
        for out_ref, chunk in jobs:
            pairs = [
                (k, order[chunk + k - 1]) for k in range(steps) if chunk + k - 1 in order
            ]
            for b in range(blocks):
                out_ref[0, :, tile_of(b)], out_ref[1, :, tile_of(b)] = correlate_block(
                    a_ref, b, pairs
                )

    by_parity("az", body)


def focus_outer(a, near, away, mids):
    cells = near.shape[2]
    return pl.pallas_call(
        focus_outer_kernel,
        out_shape=(
            jax.ShapeDtypeStruct((2, 2, CHUNK, cells), F32),
            jax.ShapeDtypeStruct((mids, 2, CHUNK, cells), F32),
        ),
        in_specs=[pl.BlockSpec(memory_space=pltpu.VMEM)] * 3,
        out_specs=(pl.BlockSpec(memory_space=pltpu.VMEM),) * 2,
        compiler_params=params(),
        name="focus_outer",
    )(a, near, away)


def focus_mid_kernel(a_ref, mid_ref, part_ref, mid_part_ref, image_ref, end_ref, sum_ref, sems):
    mids, steps, blocks = mid_part_ref.shape[0], a_ref.shape[0], a_ref.shape[1]
    order = {i + 1: lines(mid_ref, i) for i in range(mids)}
    jobs = [(mid_part_ref.at[i], sum_ref.at[i], i + 1) for i in range(mids)]
    jobs += [(part_ref.at[0], end_ref.at[0], 0), (part_ref.at[1], end_ref.at[1], mids + 1)]
    copies = []
    for i, (before_ref, out_ref, chunk) in enumerate(jobs):
        pairs = [(k, order[chunk + k - 1]) for k in range(steps) if chunk + k - 1 in order]
        for b in range(blocks):
            real, imag = correlate_block(a_ref, b, pairs)
            out_ref[0, :, tile_of(b)] = before_ref[0, :, tile_of(b)] + real
            out_ref[1, :, tile_of(b)] = before_ref[1, :, tile_of(b)] + imag
        if i < mids:
            target = image_ref.at[:, pl.ds(chunk * CHUNK, CHUNK), :]
            copies.append(pltpu.make_async_copy(out_ref, target, sems.at[i]))
            copies[-1].start()
    for copy in copies:
        copy.wait()


def focus_mid(a, mid, part, mid_part):
    cells = mid.shape[2]
    mids = mid_part.shape[0]
    return pl.pallas_call(
        focus_mid_kernel,
        out_shape=(
            jax.ShapeDtypeStruct((2, (mids + 2) * CHUNK, cells), F32),
            jax.ShapeDtypeStruct(part.shape, F32),
        ),
        in_specs=[pl.BlockSpec(memory_space=pltpu.VMEM)] * 4,
        out_specs=(pl.BlockSpec(memory_space=pl.ANY), pl.BlockSpec(memory_space=pltpu.VMEM)),
        scratch_shapes=[pltpu.VMEM(mid_part.shape, F32), pltpu.SemaphoreType.DMA((mids,))],
        compiler_params=params(),
        name="focus_mid",
    )(a, mid, part, mid_part)


def focus_end_kernel(which, a_ref, part_ref, halo_ref, _, image_ref, sum_ref, sem):
    rows = image_ref.shape[1]

    def body(odd):
        end = 1 - odd if which == "near" else odd
        for b in range(a_ref.shape[1]):
            real, imag = correlate_block(a_ref, b, [(2 * end, lines(halo_ref, 0))])
            sum_ref[0, :, tile_of(b)] = part_ref[end, 0, :, tile_of(b)] + real
            sum_ref[1, :, tile_of(b)] = part_ref[end, 1, :, tile_of(b)] + imag
        target = image_ref.at[:, pl.ds(end * (rows - CHUNK), CHUNK), :]
        copy = pltpu.make_async_copy(sum_ref, target, sem)
        copy.start()
        copy.wait()

    by_parity("az", body)


def focus_end(which, a, part, halo, image):
    return pl.pallas_call(
        functools.partial(focus_end_kernel, which),
        out_shape=jax.ShapeDtypeStruct(image.shape, F32),
        in_specs=[pl.BlockSpec(memory_space=pltpu.VMEM)] * 3
        + [pl.BlockSpec(memory_space=pl.ANY)],
        out_specs=pl.BlockSpec(memory_space=pl.ANY),
        scratch_shapes=[pltpu.VMEM(part.shape[1:], F32), pltpu.SemaphoreType.DMA],
        input_output_aliases={3: 0},
        compiler_params=params(),
        name="focus_" + which,
    )(a, part, halo, image)


def per_device(raw_echo, range_chirp, migration_taps, block_shift, azimuth_chirp):
    shifted, far_outer, far_mid, core_outer, core_mid, w, taps, splat, azimuth_chirp = range_edges(
        raw_echo, range_chirp, migration_taps, block_shift, azimuth_chirp
    )
    core_outer = swap(core_outer, "rg", 0)
    core_mid = swap(core_mid, "rg", 0)
    far_outer = swap(far_outer, "rg", 1)
    far_mid = swap(far_mid, "rg", 1)
    near, m = compress("near", shifted, core_outer, far_outer, w, taps, splat)
    near_halo = swap(near, "az", 0)
    core_outer, core_mid, near = lax.optimization_barrier((core_outer, core_mid, near))
    away = compress("away", shifted, core_outer, far_outer, w, m)
    away_halo = swap(away, "az", 1)
    away, azimuth_chirp = lax.optimization_barrier((away, azimuth_chirp))
    a = azimuth_weights(azimuth_chirp)
    part, mid_part = focus_outer(a, near, away, raw_echo.shape[1] // CHUNK - 2)
    far_mid, part = lax.optimization_barrier((far_mid, part))
    mid = compress("mid", shifted, core_mid, far_mid, w, m)
    image, part = focus_mid(a, mid, part, mid_part)
    image = focus_end("near", a, part, near_halo, image)
    return focus_end("away", a, part, away_halo, image)


def solution(mesh):
    placed = (P(None, "az", "rg"), P(), P(None, "rg"), P("rg"), P("rg", None, None))
    return jax.shard_map(
        per_device, mesh=mesh, in_specs=placed, out_specs=P(None, "az", "rg"), check_vma=False
    )
```

profile of v0, /device:TPU:12, one launch (start us, length us, event | category | flops | bytes accessed | tf_op | source)
XLA Modules:
  0.0 30.5 jit_solution(7720923665040317517)
XLA Ops:
  0.0 2.1 %range_edges.1 = (bf16[2,1024,512]{2,1,0:T(8,128)(2,1)S(1)}, bf16[2,1280,128]{2,1,0:T(8,128)(2,1)S(1)}, bf16[2,1280,128]{2,1,0:T(8,128)(2,1)S(1)}, bf16[2,1312,1...) custom-call(bf16[2,1024,384]{2,1,0:T(8,128)(2,1)} %x_hbm.1, ...), custom_call_target="tpu_custom_call" | custom-call | tf_op jit(solution)/shard_map/range_edges/pallas_call | solution.py:212
  2.1 0.1 collective-permute-start
  2.2 0.5 %collective-permute-start.1 = (bf16[2,1296,128]{2,1,0:T(8,128)(2,1)S(1)}, bf16[2,1296,128]{2,1,0:T(8,128)(2,1)S(1)}, u32[]{:S(2)}, u32[]{:S(2)}) collective-permute-start(bf16[2,1296,128]{2,1,0:T(8,128)(2,1)S(1)} %get-tuple-element.29), channel_id=1, source_target_pairs={{0,1},{1,0},{2,3},{3,2},{4,5},{5,4},{6,7},{7,6},{8,9},{9,8},{10,11... | collective-permute-start | bytes 1990664 | tf_op jit(solution)/shard_map/ppermute | solution.py:48
  2.7 2.1 %collective-permute-start.2 = (bf16[2,1280,128]{2,1,0:T(8,128)(2,1)S(1)}, bf16[2,1280,128]{2,1,0:T(8,128)(2,1)S(1)}, u32[]{:S(2)}, u32[]{:S(2)}) collective-permute-start(bf16[2,1280,128]{2,1,0:T(8,128)(2,1)S(1)} %get-tuple-element.30), channel_id=1, source_target_pairs={{1,2},{2,1},{5,6},{6,5},{9,10},{10,9},{13,14},{14,13},{17,18},{18,... | collective-permute-start | bytes 1966088 | tf_op jit(solution)/shard_map/ppermute | solution.py:48
  4.8 3.5 %collective-permute-start.3 = (bf16[2,1280,128]{2,1,0:T(8,128)(2,1)S(1)}, bf16[2,1280,128]{2,1,0:T(8,128)(2,1)S(1)}, u32[]{:S(2)}, u32[]{:S(2)}) collective-permute-start(bf16[2,1280,128]{2,1,0:T(8,128)(2,1)S(1)} %get-tuple-element.40), channel_id=1, source_target_pairs={{1,2},{2,1},{5,6},{6,5},{9,10},{10,9},{13,14},{14,13},{17,18},{18,... | collective-permute-start | bytes 1966088 | tf_op jit(solution)/shard_map/ppermute | solution.py:48
  8.2 6.3 %collective-permute-done.2.far_ref = bf16[2,1280,128]{2,1,0:T(8,128)(2,1)S(1)} collective-permute-done((bf16[2,1280,128]{2,1,0:T(8,128)(2,1)S(1)}, bf16[2,1280,128]{2,1,0:T(8,128)(2,1)S(1)}, u32[]{:S(2)}, u32[]{:S(2)}) %collective-permute-start.2) | collective-permute-done | bytes 655392 | tf_op jit(solution)/shard_map/ppermute | solution.py:48
  14.6 0.0 collective-permute-done.core_ref
  14.6 1.2 %compress_near.1 = (bf16[2,256,384]{2,1,0:T(8,128)(2,1)S(1)}, bf16[3,256,128]{2,1,0:T(8,128)(2,1)S(1)}) custom-call(bf16[2,1024,512]{2,1,0:T(8,128)(2,1)S(1)} %get-tuple-element.27.s_ref, bf16[2,1312,128]{2,1,0:T(8,128)(2,1)S(1)} %collective-permute-done.core_ref, bf16[2,1280,128]{2,1,0:T(8,128)(2,1)S(1)} %collective-permute-done.2.far_ref, ...), custom_call_target="tpu_custom_call" | custom-call | tf_op jit(solution)/shard_map/compress_near/pallas_call | solution.py:308
  15.8 1.6 %collective-permute-start.5 = (bf16[2,256,384]{2,1,0:T(8,128)(2,1)S(1)}, bf16[2,256,384]{2,1,0:T(8,128)(2,1)S(1)}, u32[]{:S(2)}, u32[]{:S(2)}) collective-permute-start(bf16[2,256,384]{2,1,0:T(8,128)(2,1)S(1)} %get-tuple-element.41.near_ref), channel_id=1, source_target_pairs={{0,4},{4,0},{8,12},{12,8},{16,20},{20,16},{24,28},{28,24},{1,5},{5... | collective-permute-start | bytes 1179656 | tf_op jit(solution)/shard_map/ppermute | solution.py:48
  17.4 0.0 collective-permute-done.1.core_ref
  17.4 1.1 %compress_away.1.away_ref = bf16[2,256,384]{2,1,0:T(8,128)(2,1)S(1)} custom-call(bf16[2,1024,512]{2,1,0:T(8,128)(2,1)S(1)} %get-tuple-element.27.s_ref, bf16[2,1312,128]{2,1,0:T(8,128)(2,1)S(1)} %collective-permute-done.core_ref, bf16[2,1280,128]{2,1,0:T(8,128)(2,1)S(1)} %collective-permute-done.2.far_ref, bf16[1280,256]{1,0:T(8,128)(2,1)S(1)} %get-tuple-element.31.w_ref, ...), custom_call_target="tpu_custom_call" | custom-call | tf_op jit(solution)/shard_map/compress_away/pallas_call | solution.py:308
  18.5 2.3 %collective-permute-start.4 = (bf16[2,256,384]{2,1,0:T(8,128)(2,1)S(1)}, bf16[2,256,384]{2,1,0:T(8,128)(2,1)S(1)}, u32[]{:S(2)}, u32[]{:S(2)}) collective-permute-start(bf16[2,256,384]{2,1,0:T(8,128)(2,1)S(1)} %compress_away.1.away_ref), channel_id=1, source_target_pairs={{4,8},{8,4},{12,16},{16,12},{20,24},{24,20},{5,9},{9,5},{13,17},{1... | collective-permute-start | bytes 1179656 | tf_op jit(solution)/shard_map/ppermute | solution.py:48
  20.9 0.3 azimuth_weights.1.a_ref
  21.2 1.0 %focus_outer.1 = (f32[2,2,256,384]{3,2,1,0:T(8,128)S(1)}, f32[2,2,256,384]{3,2,1,0:T(8,128)S(1)}) custom-call(bf16[3,3,512,256]{3,2,1,0:T(8,128)(2,1)S(1)} %azimuth_weights.1.a_ref, bf16[2,256,384]{2,1,0:T(8,128)(2,1)S(1)} %get-tuple-element.41.near_ref, bf16[2,256,384]{2,1,0:T(8,128)(2,1)S(1)} %compress_away.1.away_ref), custom_call_target="tpu_custom_call" | custom-call | tf_op jit(solution)/shard_map/focus_outer/pallas_call | solution.py:361
  22.2 0.0 collective-permute-done.3.far_ref
  22.2 2.2 %compress_mid.1.mid_ref = bf16[2,512,384]{2,1,0:T(8,128)(2,1)S(1)} custom-call(bf16[2,1024,512]{2,1,0:T(8,128)(2,1)S(1)} %get-tuple-element.27.s_ref, bf16[2,1296,128]{2,1,0:T(8,128)(2,1)S(1)} %collective-permute-done.1.core_ref, bf16[2,1280,128]{2,1,0:T(8,128)(2,1)S(1)} %collective-permute-done.3.far_ref, bf16[1280,256]{1,0:T(8,128)(2,1)S(1)} %get-tuple-element.31.w_ref, ...), custom_call_target="tpu_custom_call" | custom-call | tf_op jit(solution)/shard_map/compress_mid/pallas_call | solution.py:308
  24.4 2.0 %focus_mid.1 = (f32[2,1024,384]{2,1,0:T(8,128)}, f32[2,2,256,384]{3,2,1,0:T(8,128)S(1)}) custom-call(bf16[3,3,512,256]{3,2,1,0:T(8,128)(2,1)S(1)} %azimuth_weights.1.a_ref, bf16[2,512,384]{2,1,0:T(8,128)(2,1)S(1)} %compress_mid.1.mid_ref, f32[2,2,256,384]{3,2,1,0:T(8,128)S(1)} %get-tuple-element.45.part_ref, ...), custom_call_target="tpu_custom_call" | custom-call | tf_op jit(solution)/shard_map/focus_mid/pallas_call | solution.py:397
  26.4 0.0 collective-permute-done.5.halo_ref
  26.4 1.3 %focus_near.1._ = f32[2,1024,384]{2,1,0:T(8,128)} custom-call(bf16[3,3,512,256]{3,2,1,0:T(8,128)(2,1)S(1)} %azimuth_weights.1.a_ref, f32[2,2,256,384]{3,2,1,0:T(8,128)S(1)} %get-tuple-element.47.part_ref, bf16[2,256,384]{2,1,0:T(8,128)(2,1)S(1)} %collective-permute-done.5.halo_ref, f32[2,1024,384]{2,1,0:T(8,128)} %get-tuple-element.48._), custom_call_target="tpu_custom_call", output_to_operand_aliasing={{}: (3, {})} | custom-call | tf_op jit(solution)/shard_map/focus_near/pallas_call | solution.py:429
  27.7 1.4 %collective-permute-done.4.halo_ref = bf16[2,256,384]{2,1,0:T(8,128)(2,1)S(1)} collective-permute-done((bf16[2,256,384]{2,1,0:T(8,128)(2,1)S(1)}, bf16[2,256,384]{2,1,0:T(8,128)(2,1)S(1)}, u32[]{:S(2)}, u32[]{:S(2)}) %collective-permute-start.4) | collective-permute-done | bytes 393248 | tf_op jit(solution)/shard_map/ppermute | solution.py:48
  29.1 1.3 %focus_away.1 = f32[2,1024,384]{2,1,0:T(8,128)} custom-call(bf16[3,3,512,256]{3,2,1,0:T(8,128)(2,1)S(1)} %azimuth_weights.1.a_ref, f32[2,2,256,384]{3,2,1,0:T(8,128)S(1)} %get-tuple-element.47.part_ref, bf16[2,256,384]{2,1,0:T(8,128)(2,1)S(1)} %collective-permute-done.4.halo_ref, f32[2,1024,384]{2,1,0:T(8,128)} %focus_near.1._), custom_call_target="tpu_custom_call", output_to_operand_aliasing={{}: (3, {})} | custom-call | tf_op jit(solution)/shard_map/focus_away/pallas_call | solution.py:429
Async XLA Ops:
  2.1 12.5 %collective-permute-start = (bf16[2,1312,128]{2,1,0:T(8,128)(2,1)S(1)}, bf16[2,1312,128]{2,1,0:T(8,128)(2,1)S(1)}, u32[]{:S(2)}, u32[]{:S(2)}) collective-permute-start(bf16[2,1312,128]{2,1,0:T(8,128)(2,1)S(1)} %get-tuple-element.28), channel_id=1, source_target_pairs={{0,1},{1,0},{2,3},{3,2},{4,5},{5,4},{6,7},{7,6},{8,9},{9,8},{10,11... | collective-permute-start | bytes 2015240 | tf_op jit(solution)/shard_map/ppermute | solution.py:48
  2.2 15.2 %collective-permute-start.1 = (bf16[2,1296,128]{2,1,0:T(8,128)(2,1)S(1)}, bf16[2,1296,128]{2,1,0:T(8,128)(2,1)S(1)}, u32[]{:S(2)}, u32[]{:S(2)}) collective-permute-start(bf16[2,1296,128]{2,1,0:T(8,128)(2,1)S(1)} %get-tuple-element.29), channel_id=1, source_target_pairs={{0,1},{1,0},{2,3},{3,2},{4,5},{5,4},{6,7},{7,6},{8,9},{9,8},{10,11... | collective-permute-start | bytes 1990664 | tf_op jit(solution)/shard_map/ppermute | solution.py:48
  2.7 11.9 %collective-permute-start.2 = (bf16[2,1280,128]{2,1,0:T(8,128)(2,1)S(1)}, bf16[2,1280,128]{2,1,0:T(8,128)(2,1)S(1)}, u32[]{:S(2)}, u32[]{:S(2)}) collective-permute-start(bf16[2,1280,128]{2,1,0:T(8,128)(2,1)S(1)} %get-tuple-element.30), channel_id=1, source_target_pairs={{1,2},{2,1},{5,6},{6,5},{9,10},{10,9},{13,14},{14,13},{17,18},{18,... | collective-permute-start | bytes 1966088 | tf_op jit(solution)/shard_map/ppermute | solution.py:48
  4.8 17.4 %collective-permute-start.3 = (bf16[2,1280,128]{2,1,0:T(8,128)(2,1)S(1)}, bf16[2,1280,128]{2,1,0:T(8,128)(2,1)S(1)}, u32[]{:S(2)}, u32[]{:S(2)}) collective-permute-start(bf16[2,1280,128]{2,1,0:T(8,128)(2,1)S(1)} %get-tuple-element.40), channel_id=1, source_target_pairs={{1,2},{2,1},{5,6},{6,5},{9,10},{10,9},{13,14},{14,13},{17,18},{18,... | collective-permute-start | bytes 1966088 | tf_op jit(solution)/shard_map/ppermute | solution.py:48
  15.8 10.6 %collective-permute-start.5 = (bf16[2,256,384]{2,1,0:T(8,128)(2,1)S(1)}, bf16[2,256,384]{2,1,0:T(8,128)(2,1)S(1)}, u32[]{:S(2)}, u32[]{:S(2)}) collective-permute-start(bf16[2,256,384]{2,1,0:T(8,128)(2,1)S(1)} %get-tuple-element.41.near_ref), channel_id=1, source_target_pairs={{0,4},{4,0},{8,12},{12,8},{16,20},{20,16},{24,28},{28,24},{1,5},{5... | collective-permute-start | bytes 1179656 | tf_op jit(solution)/shard_map/ppermute | solution.py:48
  18.5 10.6 %collective-permute-start.4 = (bf16[2,256,384]{2,1,0:T(8,128)(2,1)S(1)}, bf16[2,256,384]{2,1,0:T(8,128)(2,1)S(1)}, u32[]{:S(2)}, u32[]{:S(2)}) collective-permute-start(bf16[2,256,384]{2,1,0:T(8,128)(2,1)S(1)} %compress_away.1.away_ref), channel_id=1, source_target_pairs={{4,8},{8,4},{12,16},{16,12},{20,24},{24,20},{5,9},{9,5},{13,17},{1... | collective-permute-start | bytes 1179656 | tf_op jit(solution)/shard_map/ppermute | solution.py:48
where the time goes:
time: 30.7 us; the launch traced here: 30.5 us
  Pallas kernels  12.5 us (41%)
  starting transfers between devices  10 us (33%)
  waiting for transfers between devices  7.7 us (25%)
    ppermute x6, starting transfers between devices, swap(): return lax.ppermute(x, axis, swap_pairs(lax.axis_size(axis), first))  10 us
    ppermute x6, waiting for transfers between devices, swap(): return lax.ppermute(x, axis, swap_pairs(lax.axis_size(axis), first))  7.7 us
    pallas_call x3, Pallas kernels, compress(): pl.pallas_call(functools.partial(compress_kernel, which), out_shape=out,...  4.62 us
    pallas_call x2, Pallas kernels, focus_end(): pl.pallas_call(functools.partial(focus_end_kernel, which), out_shape=jax....  2.54 us
    pallas_call x1, Pallas kernels, range_edges(): pl.pallas_call(edges_kernel, out_shape=(jax.ShapeDtypeStruct(raw.shape[:2...  2.1 us
    pallas_call x1, Pallas kernels, focus_mid(): pl.pallas_call(focus_mid_kernel, out_shape=(jax.ShapeDtypeStruct((2, (mid...  1.98 us
    pallas_call x1, Pallas kernels, focus_outer(): pl.pallas_call(focus_outer_kernel, out_shape=(jax.ShapeDtypeStruct((2, 2,...  1.01 us
  transfers between devices with their start and end apart: 6, of which 2 were waited for; matrix products, arithmetic and copies ran while one was open for 0% of the time, Pallas kernels for 30%

commit v1 on v0

--- a/solution.py
+++ b/solution.py
@@ -161,7 +161,7 @@
 
 def edges_kernel(
     x_hbm, range_hbm, taps_hbm, shift_hbm, azimuth_hbm,
-    s_ref, far_outer_ref, far_mid_ref, core_outer_ref, core_mid_ref,
+    s_ref, far_near_ref, far_away_ref, far_mid_ref, core_outer_ref, core_mid_ref,
     w_ref, taps_ref, splat_ref, azimuth_ref, x_ref, range_ref, shift_ref, sems,
 ):
     rows = x_ref.shape[1]
@@ -175,9 +175,8 @@
     ]
     small = len(moves)
     for start in starts:
-        for part in range(2):
-            picked = pl.ds(start, CHUNK)
-            moves.append((x_hbm.at[part, picked, :], x_ref.at[part, picked, :]))
+        picked = pl.ds(start, CHUNK)
+        moves.append((x_hbm.at[:, picked, :], x_ref.at[:, picked, :]))
     copies = [
         pltpu.make_async_copy(source, target, sems.at[i])
         for i, (source, target) in enumerate(moves)
@@ -195,11 +194,10 @@
 
     def body(odd):
         for i, start in enumerate(starts):
-            copies[small + 2 * i].wait()
-            copies[small + 2 * i + 1].wait()
-            outer = (core_outer_ref, far_outer_ref, i)
-            core_ref, far_ref, chunk = outer if i < 2 else (core_mid_ref, far_mid_ref, i - 2)
-            edge_chunk(x_ref, s_ref, start, [(core_ref, chunk, 1 - odd), (far_ref, chunk, odd)])
+            copies[small + i].wait()
+            far = [(far_near_ref, 0), (far_away_ref, 0)][i] if i < 2 else (far_mid_ref, i - 2)
+            core = (core_outer_ref, i) if i < 2 else (core_mid_ref, i - 2)
+            edge_chunk(x_ref, s_ref, start, [core + (1 - odd,), far + (odd,)])
 
     by_parity("rg", body)
 
@@ -214,7 +212,7 @@
         out_shape=(jax.ShapeDtypeStruct(raw.shape[:2] + (raw.shape[2] + LANES,), BF16),)
         + tuple(
             jax.ShapeDtypeStruct((n, 5 * CHUNK + extra, LANES), BF16)
-            for n, extra in ((2, 0), (chunks - 2, 0), (2, 2 * PAD), (chunks - 2, PAD))
+            for n, extra in ((1, 0), (1, 0), (chunks - 2, 0), (2, 2 * PAD), (chunks - 2, PAD))
         )
         + (
             jax.ShapeDtypeStruct((2 * depth, 2 * LANES), BF16),
@@ -223,12 +221,12 @@
             jax.ShapeDtypeStruct(azimuth_chirp.shape, BF16),
         ),
         in_specs=[pl.BlockSpec(memory_space=pltpu.HBM)] * len(args),
-        out_specs=(pl.BlockSpec(memory_space=pltpu.VMEM),) * 9,
+        out_specs=(pl.BlockSpec(memory_space=pltpu.VMEM),) * 10,
         scratch_shapes=[
             pltpu.VMEM(raw.shape, BF16),
             pltpu.VMEM(range_chirp.shape, BF16),
             pltpu.SMEM(block_shift.shape, jnp.int32),
-            pltpu.SemaphoreType.DMA((2 * chunks + len(args) - 1,)),
+            pltpu.SemaphoreType.DMA((chunks + len(args) - 1,)),
         ],
         compiler_params=params(),
         name="range_edges",
@@ -289,7 +287,7 @@
         if which == "near":
             migration_bands(taps_ref, splat_ref, m_ref)
         for i, (start, chunk) in enumerate(jobs):
-            core, far = (core_ref, chunk), (far_ref, chunk)
+            core, far = (core_ref, chunk), (far_ref, chunk if which == "mid" else 0)
             left, right = (core, far) if odd else (far, core)
             compress_chunk(
                 s_ref, start, left, right, w_ref, m_ref, out_ref, i * CHUNK, c_refs[i]
@@ -408,49 +406,72 @@
     )(a, mid, part, mid_part)
 
 
-def focus_end_kernel(which, a_ref, part_ref, halo_ref, _, image_ref, sum_ref, sem):
+def add_halo(a_ref, end, part_ref, halo_ref, out_ref):
+    for b in range(a_ref.shape[1]):
+        real, imag = correlate_block(a_ref, b, [(2 * end, lines(halo_ref, 0))])
+        out_ref[0, :, tile_of(b)] = part_ref[end, 0, :, tile_of(b)] + real
+        out_ref[1, :, tile_of(b)] = part_ref[end, 1, :, tile_of(b)] + imag
+
+
+def near_end_kernel(a_ref, part_ref, halo_ref, out_ref):
+    by_parity("az", lambda odd: add_halo(a_ref, 1 - odd, part_ref, halo_ref, out_ref))
+
+
+def near_end(a, part, halo):
+    return pl.pallas_call(
+        near_end_kernel,
+        out_shape=jax.ShapeDtypeStruct(part.shape[1:], F32),
+        in_specs=[pl.BlockSpec(memory_space=pltpu.VMEM)] * 3,
+        out_specs=pl.BlockSpec(memory_space=pltpu.VMEM),
+        compiler_params=params(),
+        name="near_end",
+    )(a, part, halo)
+
+
+def ends_kernel(a_ref, part_ref, near_ref, halo_ref, _, image_ref, sum_ref, sems):
     rows = image_ref.shape[1]
 
     def body(odd):
-        end = 1 - odd if which == "near" else odd
-        for b in range(a_ref.shape[1]):
-            real, imag = correlate_block(a_ref, b, [(2 * end, lines(halo_ref, 0))])
-            sum_ref[0, :, tile_of(b)] = part_ref[end, 0, :, tile_of(b)] + real
-            sum_ref[1, :, tile_of(b)] = part_ref[end, 1, :, tile_of(b)] + imag
-        target = image_ref.at[:, pl.ds(end * (rows - CHUNK), CHUNK), :]
-        copy = pltpu.make_async_copy(sum_ref, target, sem)
-        copy.start()
-        copy.wait()
+        copies = []
+        for i, (source, end) in enumerate(((near_ref, 1 - odd), (sum_ref, odd))):
+            if i == 1:
+                add_halo(a_ref, end, part_ref, halo_ref, sum_ref)
+            target = image_ref.at[:, pl.ds(end * (rows - CHUNK), CHUNK), :]
+            copies.append(pltpu.make_async_copy(source, target, sems.at[i]))
+            copies[-1].start()
+        for copy in copies:
+            copy.wait()
 
     by_parity("az", body)
 
 
-def focus_end(which, a, part, halo, image):
-    return pl.pallas_call(
-        functools.partial(focus_end_kernel, which),
+def ends(a, part, near, halo, image):
+    return pl.pallas_call(
+        ends_kernel,
         out_shape=jax.ShapeDtypeStruct(image.shape, F32),
-        in_specs=[pl.BlockSpec(memory_space=pltpu.VMEM)] * 3
+        in_specs=[pl.BlockSpec(memory_space=pltpu.VMEM)] * 4
         + [pl.BlockSpec(memory_space=pl.ANY)],
         out_specs=pl.BlockSpec(memory_space=pl.ANY),
-        scratch_shapes=[pltpu.VMEM(part.shape[1:], F32), pltpu.SemaphoreType.DMA],
-        input_output_aliases={3: 0},
-        compiler_params=params(),
-        name="focus_" + which,
-    )(a, part, halo, image)
+        scratch_shapes=[pltpu.VMEM(near.shape, F32), pltpu.SemaphoreType.DMA((2,))],
+        input_output_aliases={4: 0},
+        compiler_params=params(),
+        name="ends",
+    )(a, part, near, halo, image)
 
 
 def per_device(raw_echo, range_chirp, migration_taps, block_shift, azimuth_chirp):
-    shifted, far_outer, far_mid, core_outer, core_mid, w, taps, splat, azimuth_chirp = range_edges(
+    shifted, far_near, far_away, far_mid, core_outer, core_mid, w, taps, splat, azimuth_chirp = range_edges(
         raw_echo, range_chirp, migration_taps, block_shift, azimuth_chirp
     )
     core_outer = swap(core_outer, "rg", 0)
     core_mid = swap(core_mid, "rg", 0)
-    far_outer = swap(far_outer, "rg", 1)
+    far_near = swap(far_near, "rg", 1)
+    far_away = swap(far_away, "rg", 1)
     far_mid = swap(far_mid, "rg", 1)
-    near, m = compress("near", shifted, core_outer, far_outer, w, taps, splat)
+    near, m = compress("near", shifted, core_outer, far_near, w, taps, splat)
     near_halo = swap(near, "az", 0)
     core_outer, core_mid, near = lax.optimization_barrier((core_outer, core_mid, near))
-    away = compress("away", shifted, core_outer, far_outer, w, m)
+    away = compress("away", shifted, core_outer, far_away, w, m)
     away_halo = swap(away, "az", 1)
     away, azimuth_chirp = lax.optimization_barrier((away, azimuth_chirp))
     a = azimuth_weights(azimuth_chirp)
@@ -458,8 +479,7 @@
     far_mid, part = lax.optimization_barrier((far_mid, part))
     mid = compress("mid", shifted, core_mid, far_mid, w, m)
     image, part = focus_mid(a, mid, part, mid_part)
-    image = focus_end("near", a, part, near_halo, image)
-    return focus_end("away", a, part, away_halo, image)
+    return ends(a, part, near_end(a, part, near_halo), away_halo, image)
 
 
 def solution(mesh):

time: 30.7 us -> 29.7 us (0.967)
  the two profiles are of different devices: /device:TPU:12 before, /device:TPU:17 now
where the time goes in v1:
time: 29.7 us; the launch traced here: 29.5 us
  starting transfers between devices  14.4 us (48%)
  Pallas kernels  11.4 us (38%)
  waiting for transfers between devices  3.41 us (11%)
    ppermute x7, starting transfers between devices, swap(): return lax.ppermute(x, axis, swap_pairs(lax.axis_size(axis), first))  14.4 us
    pallas_call x3, Pallas kernels, compress(): pl.pallas_call(functools.partial(compress_kernel, which), out_shape=out,...  4.44 us
    ppermute x7, waiting for transfers between devices, swap(): return lax.ppermute(x, axis, swap_pairs(lax.axis_size(axis), first))  3.41 us
    pallas_call x1, Pallas kernels, range_edges(): pl.pallas_call(edges_kernel, out_shape=(jax.ShapeDtypeStruct(raw.shape[:2...  2.05 us
    pallas_call x1, Pallas kernels, focus_mid(): pl.pallas_call(focus_mid_kernel, out_shape=(jax.ShapeDtypeStruct((2, (mid...  1.99 us
    pallas_call x1, Pallas kernels, ends(): pl.pallas_call(ends_kernel, out_shape=jax.ShapeDtypeStruct(image.shape, F...  1.3 us
    pallas_call x1, Pallas kernels, focus_outer(): pl.pallas_call(focus_outer_kernel, out_shape=(jax.ShapeDtypeStruct((2, 2,...  1 us
  transfers between devices with their start and end apart: 7, of which 3 were waited for; matrix products, arithmetic and copies ran while one was open for 0% of the time, Pallas kernels for 27%

profile of v1, /device:TPU:17, one launch (start us, length us, event | category | flops | bytes accessed | tf_op | source)
XLA Modules:
  0.0 29.5 jit_solution(11929464280871474025)
XLA Ops:
  0.0 2.1 %range_edges.1 = (bf16[2,1024,512]{2,1,0:T(8,128)(2,1)S(1)}, bf16[1,1280,128]{2,1,0:T(8,128)(2,1)S(1)}, bf16[1,1280,128]{2,1,0:T(8,128)(2,1)S(1)}, bf16[2,1280,1...) custom-call(bf16[2,1024,384]{2,1,0:T(8,128)(2,1)} %x_hbm.1, ...), custom_call_target="tpu_custom_call" | custom-call | tf_op jit(solution)/shard_map/range_edges/pallas_call | solution.py:210
  2.1 0.7 %collective-permute-start = (bf16[2,1312,128]{2,1,0:T(8,128)(2,1)S(1)}, bf16[2,1312,128]{2,1,0:T(8,128)(2,1)S(1)}, u32[]{:S(2)}, u32[]{:S(2)}) collective-permute-start(bf16[2,1312,128]{2,1,0:T(8,128)(2,1)S(1)} %get-tuple-element.29), channel_id=1, source_target_pairs={{0,1},{1,0},{2,3},{3,2},{4,5},{5,4},{6,7},{7,6},{8,9},{9,8},{10,11... | collective-permute-start | bytes 2015240 | tf_op jit(solution)/shard_map/ppermute | solution.py:48
  2.8 0.1 collective-permute-start.1
  2.9 3.5 %collective-permute-start.2 = (bf16[1,1280,128]{2,1,0:T(8,128)(2,1)S(1)}, bf16[1,1280,128]{2,1,0:T(8,128)(2,1)S(1)}, u32[]{:S(2)}, u32[]{:S(2)}) collective-permute-start(bf16[1,1280,128]{2,1,0:T(8,128)(2,1)S(1)} %get-tuple-element.31), channel_id=1, source_target_pairs={{1,2},{2,1},{5,6},{6,5},{9,10},{10,9},{13,14},{14,13},{17,18},{18,... | collective-permute-start | bytes 983048 | tf_op jit(solution)/shard_map/ppermute | solution.py:48
  6.3 2.1 %collective-permute-start.3 = (bf16[1,1280,128]{2,1,0:T(8,128)(2,1)S(1)}, bf16[1,1280,128]{2,1,0:T(8,128)(2,1)S(1)}, u32[]{:S(2)}, u32[]{:S(2)}) collective-permute-start(bf16[1,1280,128]{2,1,0:T(8,128)(2,1)S(1)} %get-tuple-element.37), channel_id=1, source_target_pairs={{1,2},{2,1},{5,6},{6,5},{9,10},{10,9},{13,14},{14,13},{17,18},{18,... | collective-permute-start | bytes 983048 | tf_op jit(solution)/shard_map/ppermute | solution.py:48
  8.4 3.5 %collective-permute-start.4 = (bf16[2,1280,128]{2,1,0:T(8,128)(2,1)S(1)}, bf16[2,1280,128]{2,1,0:T(8,128)(2,1)S(1)}, u32[]{:S(2)}, u32[]{:S(2)}) collective-permute-start(bf16[2,1280,128]{2,1,0:T(8,128)(2,1)S(1)} %get-tuple-element.42), channel_id=1, source_target_pairs={{1,2},{2,1},{5,6},{6,5},{9,10},{10,9},{13,14},{14,13},{17,18},{18,... | collective-permute-start | bytes 1966088 | tf_op jit(solution)/shard_map/ppermute | solution.py:48
  11.9 0.0 collective-permute-done.2.far_ref
  11.9 0.0 collective-permute-done.core_ref
  11.9 1.3 %compress_near.1 = (bf16[2,256,384]{2,1,0:T(8,128)(2,1)S(1)}, bf16[3,256,128]{2,1,0:T(8,128)(2,1)S(1)}) custom-call(bf16[2,1024,512]{2,1,0:T(8,128)(2,1)S(1)} %get-tuple-element.28.s_ref, bf16[2,1312,128]{2,1,0:T(8,128)(2,1)S(1)} %collective-permute-done.core_ref, bf16[1,1280,128]{2,1,0:T(8,128)(2,1)S(1)} %collective-permute-done.2.far_ref, ...), custom_call_target="tpu_custom_call" | custom-call | tf_op jit(solution)/shard_map/compress_near/pallas_call | solution.py:306
  13.2 1.3 %collective-permute-start.5 = (bf16[2,256,384]{2,1,0:T(8,128)(2,1)S(1)}, bf16[2,256,384]{2,1,0:T(8,128)(2,1)S(1)}, u32[]{:S(2)}, u32[]{:S(2)}) collective-permute-start(bf16[2,256,384]{2,1,0:T(8,128)(2,1)S(1)} %get-tuple-element.43.near_ref), channel_id=1, source_target_pairs={{0,4},{4,0},{8,12},{12,8},{16,20},{20,16},{24,28},{28,24},{1,5},{5... | collective-permute-start | bytes 1179656 | tf_op jit(solution)/shard_map/ppermute | solution.py:48
  14.5 0.0 collective-permute-done.1.core_ref
  14.5 0.3 %collective-permute-done.3.far_ref = bf16[1,1280,128]{2,1,0:T(8,128)(2,1)S(1)} collective-permute-done((bf16[1,1280,128]{2,1,0:T(8,128)(2,1)S(1)}, bf16[1,1280,128]{2,1,0:T(8,128)(2,1)S(1)}, u32[]{:S(2)}, u32[]{:S(2)}) %collective-permute-start.3) | collective-permute-done | bytes 327712 | tf_op jit(solution)/shard_map/ppermute | solution.py:48
  14.8 1.1 %compress_away.1.away_ref = bf16[2,256,384]{2,1,0:T(8,128)(2,1)S(1)} custom-call(bf16[2,1024,512]{2,1,0:T(8,128)(2,1)S(1)} %get-tuple-element.28.s_ref, bf16[2,1312,128]{2,1,0:T(8,128)(2,1)S(1)} %collective-permute-done.core_ref, bf16[1,1280,128]{2,1,0:T(8,128)(2,1)S(1)} %collective-permute-done.3.far_ref, bf16[1280,256]{1,0:T(8,128)(2,1)S(1)} %get-tuple-element.32.w_ref, ...), custom_call_target="tpu_custom_call" | custom-call | tf_op jit(solution)/shard_map/compress_away/pallas_call | solution.py:306
  15.9 3.3 %collective-permute-start.6 = (bf16[2,256,384]{2,1,0:T(8,128)(2,1)S(1)}, bf16[2,256,384]{2,1,0:T(8,128)(2,1)S(1)}, u32[]{:S(2)}, u32[]{:S(2)}) collective-permute-start(bf16[2,256,384]{2,1,0:T(8,128)(2,1)S(1)} %compress_away.1.away_ref), channel_id=1, source_target_pairs={{4,8},{8,4},{12,16},{16,12},{20,24},{24,20},{5,9},{9,5},{13,17},{1... | collective-permute-start | bytes 1179656 | tf_op jit(solution)/shard_map/ppermute | solution.py:48
  19.2 0.3 %azimuth_weights.1.a_ref = bf16[3,3,512,256]{3,2,1,0:T(8,128)(2,1)S(1)} custom-call(bf16[3,2,512]{2,1,0:T(2,128)(2,1)S(1)} %get-tuple-element.40.azimuth_ref), custom_call_target="tpu_custom_call" | custom-call | tf_op jit(solution)/shard_map/azimuth_weights/pallas_call | solution.py:114
  19.5 1.0 %focus_outer.1 = (f32[2,2,256,384]{3,2,1,0:T(8,128)S(1)}, f32[2,2,256,384]{3,2,1,0:T(8,128)S(1)}) custom-call(bf16[3,3,512,256]{3,2,1,0:T(8,128)(2,1)S(1)} %azimuth_weights.1.a_ref, bf16[2,256,384]{2,1,0:T(8,128)(2,1)S(1)} %get-tuple-element.43.near_ref, bf16[2,256,384]{2,1,0:T(8,128)(2,1)S(1)} %compress_away.1.away_ref), custom_call_target="tpu_custom_call" | custom-call | tf_op jit(solution)/shard_map/focus_outer/pallas_call | solution.py:359
  20.5 1.3 %collective-permute-done.4.far_ref = bf16[2,1280,128]{2,1,0:T(8,128)(2,1)S(1)} collective-permute-done((bf16[2,1280,128]{2,1,0:T(8,128)(2,1)S(1)}, bf16[2,1280,128]{2,1,0:T(8,128)(2,1)S(1)}, u32[]{:S(2)}, u32[]{:S(2)}) %collective-permute-start.4) | collective-permute-done | bytes 655392 | tf_op jit(solution)/shard_map/ppermute | solution.py:48
  21.8 2.0 %compress_mid.1.mid_ref = bf16[2,512,384]{2,1,0:T(8,128)(2,1)S(1)} custom-call(bf16[2,1024,512]{2,1,0:T(8,128)(2,1)S(1)} %get-tuple-element.28.s_ref, bf16[2,1296,128]{2,1,0:T(8,128)(2,1)S(1)} %collective-permute-done.1.core_ref, bf16[2,1280,128]{2,1,0:T(8,128)(2,1)S(1)} %collective-permute-done.4.far_ref, bf16[1280,256]{1,0:T(8,128)(2,1)S(1)} %get-tuple-element.32.w_ref, ...), custom_call_target="tpu_custom_call" | custom-call | tf_op jit(solution)/shard_map/compress_mid/pallas_call | solution.py:306
  23.8 2.0 %focus_mid.1 = (f32[2,1024,384]{2,1,0:T(8,128)}, f32[2,2,256,384]{3,2,1,0:T(8,128)S(1)}) custom-call(bf16[3,3,512,256]{3,2,1,0:T(8,128)(2,1)S(1)} %azimuth_weights.1.a_ref, bf16[2,512,384]{2,1,0:T(8,128)(2,1)S(1)} %compress_mid.1.mid_ref, f32[2,2,256,384]{3,2,1,0:T(8,128)S(1)} %get-tuple-element.47.part_ref, ...), custom_call_target="tpu_custom_call" | custom-call | tf_op jit(solution)/shard_map/focus_mid/pallas_call | solution.py:395
  25.8 1.8 %collective-permute-done.5.halo_ref = bf16[2,256,384]{2,1,0:T(8,128)(2,1)S(1)} collective-permute-done((bf16[2,256,384]{2,1,0:T(8,128)(2,1)S(1)}, bf16[2,256,384]{2,1,0:T(8,128)(2,1)S(1)}, u32[]{:S(2)}, u32[]{:S(2)}) %collective-permute-start.5) | collective-permute-done | bytes 393248 | tf_op jit(solution)/shard_map/ppermute | solution.py:48
  27.7 0.4 %near_end.1.near_ref = f32[2,256,384]{2,1,0:T(8,128)S(1)} custom-call(bf16[3,3,512,256]{3,2,1,0:T(8,128)(2,1)S(1)} %azimuth_weights.1.a_ref, f32[2,2,256,384]{3,2,1,0:T(8,128)S(1)} %get-tuple-element.49.part_ref, bf16[2,256,384]{2,1,0:T(8,128)(2,1)S(1)} %collective-permute-done.5.halo_ref), custom_call_target="tpu_custom_call" | custom-call | tf_op jit(solution)/shard_map/near_end/pallas_call | solution.py:421
  28.1 0.0 collective-permute-done.6.halo_ref
  28.1 1.3 %ends.1 = f32[2,1024,384]{2,1,0:T(8,128)} custom-call(bf16[3,3,512,256]{3,2,1,0:T(8,128)(2,1)S(1)} %azimuth_weights.1.a_ref, f32[2,2,256,384]{3,2,1,0:T(8,128)S(1)} %get-tuple-element.49.part_ref, f32[2,256,384]{2,1,0:T(8,128)S(1)} %near_end.1.near_ref, bf16[2,256,384]{2,1,0:T(8,128)(2,1)S(1)} %collective-permute-done.6.halo_ref, ...), custom_call_target="tpu_custom_call", output_to_operand_aliasing={{}: (4, {})} | custom-call | tf_op jit(solution)/shard_map/ends/pallas_call | solution.py:449
Async XLA Ops:
  2.1 9.9 %collective-permute-start = (bf16[2,1312,128]{2,1,0:T(8,128)(2,1)S(1)}, bf16[2,1312,128]{2,1,0:T(8,128)(2,1)S(1)}, u32[]{:S(2)}, u32[]{:S(2)}) collective-permute-start(bf16[2,1312,128]{2,1,0:T(8,128)(2,1)S(1)} %get-tuple-element.29), channel_id=1, source_target_pairs={{0,1},{1,0},{2,3},{3,2},{4,5},{5,4},{6,7},{7,6},{8,9},{9,8},{10,11... | collective-permute-start | bytes 2015240 | tf_op jit(solution)/shard_map/ppermute | solution.py:48
  2.8 11.7 %collective-permute-start.1 = (bf16[2,1296,128]{2,1,0:T(8,128)(2,1)S(1)}, bf16[2,1296,128]{2,1,0:T(8,128)(2,1)S(1)}, u32[]{:S(2)}, u32[]{:S(2)}) collective-permute-start(bf16[2,1296,128]{2,1,0:T(8,128)(2,1)S(1)} %get-tuple-element.30), channel_id=1, source_target_pairs={{0,1},{1,0},{2,3},{3,2},{4,5},{5,4},{6,7},{7,6},{8,9},{9,8},{10,11... | collective-permute-start | bytes 1990664 | tf_op jit(solution)/shard_map/ppermute | solution.py:48
  2.9 9.0 %collective-permute-start.2 = (bf16[1,1280,128]{2,1,0:T(8,128)(2,1)S(1)}, bf16[1,1280,128]{2,1,0:T(8,128)(2,1)S(1)}, u32[]{:S(2)}, u32[]{:S(2)}) collective-permute-start(bf16[1,1280,128]{2,1,0:T(8,128)(2,1)S(1)} %get-tuple-element.31), channel_id=1, source_target_pairs={{1,2},{2,1},{5,6},{6,5},{9,10},{10,9},{13,14},{14,13},{17,18},{18,... | collective-permute-start | bytes 983048 | tf_op jit(solution)/shard_map/ppermute | solution.py:48
  6.3 8.4 %collective-permute-start.3 = (bf16[1,1280,128]{2,1,0:T(8,128)(2,1)S(1)}, bf16[1,1280,128]{2,1,0:T(8,128)(2,1)S(1)}, u32[]{:S(2)}, u32[]{:S(2)}) collective-permute-start(bf16[1,1280,128]{2,1,0:T(8,128)(2,1)S(1)} %get-tuple-element.37), channel_id=1, source_target_pairs={{1,2},{2,1},{5,6},{6,5},{9,10},{10,9},{13,14},{14,13},{17,18},{18,... | collective-permute-start | bytes 983048 | tf_op jit(solution)/shard_map/ppermute | solution.py:48
  8.4 13.3 %collective-permute-start.4 = (bf16[2,1280,128]{2,1,0:T(8,128)(2,1)S(1)}, bf16[2,1280,128]{2,1,0:T(8,128)(2,1)S(1)}, u32[]{:S(2)}, u32[]{:S(2)}) collective-permute-start(bf16[2,1280,128]{2,1,0:T(8,128)(2,1)S(1)} %get-tuple-element.42), channel_id=1, source_target_pairs={{1,2},{2,1},{5,6},{6,5},{9,10},{10,9},{13,14},{14,13},{17,18},{18,... | collective-permute-start | bytes 1966088 | tf_op jit(solution)/shard_map/ppermute | solution.py:48
  13.2 14.5 %collective-permute-start.5 = (bf16[2,256,384]{2,1,0:T(8,128)(2,1)S(1)}, bf16[2,256,384]{2,1,0:T(8,128)(2,1)S(1)}, u32[]{:S(2)}, u32[]{:S(2)}) collective-permute-start(bf16[2,256,384]{2,1,0:T(8,128)(2,1)S(1)} %get-tuple-element.43.near_ref), channel_id=1, source_target_pairs={{0,4},{4,0},{8,12},{12,8},{16,20},{20,16},{24,28},{28,24},{1,5},{5... | collective-permute-start | bytes 1179656 | tf_op jit(solution)/shard_map/ppermute | solution.py:48
  15.9 12.2 %collective-permute-start.6 = (bf16[2,256,384]{2,1,0:T(8,128)(2,1)S(1)}, bf16[2,256,384]{2,1,0:T(8,128)(2,1)S(1)}, u32[]{:S(2)}, u32[]{:S(2)}) collective-permute-start(bf16[2,256,384]{2,1,0:T(8,128)(2,1)S(1)} %compress_away.1.away_ref), channel_id=1, source_target_pairs={{4,8},{8,4},{12,16},{16,12},{20,24},{24,20},{5,9},{9,5},{13,17},{1... | collective-permute-start | bytes 1179656 | tf_op jit(solution)/shard_map/ppermute | solution.py:48

commit v2 on v1

--- a/solution.py
+++ b/solution.py
@@ -167,23 +167,23 @@
     rows = x_ref.shape[1]
     near, away = near_away_rows(rows)
     starts = [near, away] + list(range(CHUNK, rows - CHUNK, CHUNK))
-    moves = [
-        (range_hbm, range_ref),
-        (taps_hbm, taps_ref),
-        (shift_hbm, shift_ref),
-        (azimuth_hbm, azimuth_ref),
-    ]
-    small = len(moves)
+    moves = []
     for start in starts:
         picked = pl.ds(start, CHUNK)
         moves.append((x_hbm.at[:, picked, :], x_ref.at[:, picked, :]))
+    moves += [
+        (range_hbm, range_ref),
+        (shift_hbm, shift_ref),
+        (taps_hbm, taps_ref),
+        (azimuth_hbm, azimuth_ref),
+    ]
     copies = [
         pltpu.make_async_copy(source, target, sems.at[i])
         for i, (source, target) in enumerate(moves)
     ]
     for copy in copies:
         copy.start()
-    for copy in copies[:small]:
+    for copy in copies[len(starts) :]:
         copy.wait()
     for ref in (core_outer_ref, core_mid_ref):
         extra = ref.shape[1] - 5 * CHUNK
@@ -194,7 +194,7 @@
 
     def body(odd):
         for i, start in enumerate(starts):
-            copies[small + i].wait()
+            copies[i].wait()
             far = [(far_near_ref, 0), (far_away_ref, 0)][i] if i < 2 else (far_mid_ref, i - 2)
             core = (core_outer_ref, i) if i < 2 else (core_mid_ref, i - 2)
             edge_chunk(x_ref, s_ref, start, [core + (1 - odd,), far + (odd,)])
@@ -430,14 +430,33 @@
 
 def ends_kernel(a_ref, part_ref, near_ref, halo_ref, _, image_ref, sum_ref, sems):
     rows = image_ref.shape[1]
+    half = CHUNK // 2
 
     def body(odd):
-        copies = []
-        for i, (source, end) in enumerate(((near_ref, 1 - odd), (sum_ref, odd))):
-            if i == 1:
-                add_halo(a_ref, end, part_ref, halo_ref, sum_ref)
-            target = image_ref.at[:, pl.ds(end * (rows - CHUNK), CHUNK), :]
-            copies.append(pltpu.make_async_copy(source, target, sems.at[i]))
+        near_first, away_first = (1 - odd) * (rows - CHUNK), odd * (rows - CHUNK)
+        copies = [
+            pltpu.make_async_copy(
+                near_ref, image_ref.at[:, pl.ds(near_first, CHUNK), :], sems.at[2]
+            )
+        ]
+        copies[0].start()
+        window = lines(halo_ref, 0)
+        for h in range(2):
+            picked = slice(h * half, (h + 1) * half)
+            for b in range(a_ref.shape[1]):
+                taps = jnp.concatenate(
+                    [a_ref[2 * odd, b, base + h * half : base + (h + 1) * half] for base in (0, CHUNK)],
+                    axis=0,
+                )
+                both = jnp.concatenate([window(0, tile_of(b)), window(1, tile_of(b))], axis=1)
+                result = jnp.dot(taps, both, preferred_element_type=F32)
+                top, bottom = result[:half], result[half:]
+                real = top[:, :LANES] + bottom[:, LANES:]
+                imag = top[:, LANES:] - bottom[:, :LANES]
+                sum_ref[0, picked, tile_of(b)] = part_ref[odd, 0, picked, tile_of(b)] + real
+                sum_ref[1, picked, tile_of(b)] = part_ref[odd, 1, picked, tile_of(b)] + imag
+            target = image_ref.at[:, pl.ds(away_first + h * half, half), :]
+            copies.append(pltpu.make_async_copy(sum_ref.at[:, picked, :], target, sems.at[h]))
             copies[-1].start()
         for copy in copies:
             copy.wait()
@@ -452,7 +471,7 @@
         in_specs=[pl.BlockSpec(memory_space=pltpu.VMEM)] * 4
         + [pl.BlockSpec(memory_space=pl.ANY)],
         out_specs=pl.BlockSpec(memory_space=pl.ANY),
-        scratch_shapes=[pltpu.VMEM(near.shape, F32), pltpu.SemaphoreType.DMA((2,))],
+        scratch_shapes=[pltpu.VMEM(near.shape, F32), pltpu.SemaphoreType.DMA((3,))],
         input_output_aliases={4: 0},
         compiler_params=params(),
         name="ends",

time: 29.7 us -> 30.1 us (1.013)
  Pallas kernels: 11.4 us -> 11.8 us
    pallas_call x1, Pallas kernels: 2.05 us -> 2.45 us  [range_edges(): pl.pallas_call(edges_kernel, out_shape=(jax.ShapeDtypeStruct(raw.shape[:2...]
where the time goes in v2:
time: 30.1 us; the launch traced here: 29.9 us
  starting transfers between devices  14.4 us (48%)
  Pallas kernels  11.8 us (39%)
  waiting for transfers between devices  3.41 us (11%)
    ppermute x7, starting transfers between devices, swap(): return lax.ppermute(x, axis, swap_pairs(lax.axis_size(axis), first))  14.4 us
    pallas_call x3, Pallas kernels, compress(): pl.pallas_call(functools.partial(compress_kernel, which), out_shape=out,...  4.44 us
    ppermute x7, waiting for transfers between devices, swap(): return lax.ppermute(x, axis, swap_pairs(lax.axis_size(axis), first))  3.41 us
    pallas_call x1, Pallas kernels, range_edges(): pl.pallas_call(edges_kernel, out_shape=(jax.ShapeDtypeStruct(raw.shape[:2...  2.45 us
    pallas_call x1, Pallas kernels, focus_mid(): pl.pallas_call(focus_mid_kernel, out_shape=(jax.ShapeDtypeStruct((2, (mid...  1.98 us
    pallas_call x1, Pallas kernels, ends(): pl.pallas_call(ends_kernel, out_shape=jax.ShapeDtypeStruct(image.shape, F...  1.23 us
    pallas_call x1, Pallas kernels, focus_outer(): pl.pallas_call(focus_outer_kernel, out_shape=(jax.ShapeDtypeStruct((2, 2,...  1 us
  transfers between devices with their start and end apart: 7, of which 3 were waited for; matrix products, arithmetic and copies ran while one was open for 0% of the time, Pallas kernels for 27%

profile of v2, /device:TPU:17, one launch (start us, length us, event | category | flops | bytes accessed | tf_op | source)
XLA Modules:
  0.0 29.9 jit_solution(1317718566783619606)
XLA Ops:
  0.0 2.5 %range_edges.1 = (bf16[2,1024,512]{2,1,0:T(8,128)(2,1)S(1)}, bf16[1,1280,128]{2,1,0:T(8,128)(2,1)S(1)}, bf16[1,1280,128]{2,1,0:T(8,128)(2,1)S(1)}, bf16[2,1280,1...) custom-call(bf16[2,1024,384]{2,1,0:T(8,128)(2,1)} %x_hbm.1, ...), custom_call_target="tpu_custom_call" | custom-call | tf_op jit(solution)/shard_map/range_edges/pallas_call | solution.py:210
  2.5 0.7 %collective-permute-start = (bf16[2,1312,128]{2,1,0:T(8,128)(2,1)S(1)}, bf16[2,1312,128]{2,1,0:T(8,128)(2,1)S(1)}, u32[]{:S(2)}, u32[]{:S(2)}) collective-permute-start(bf16[2,1312,128]{2,1,0:T(8,128)(2,1)S(1)} %get-tuple-element.29), channel_id=1, source_target_pairs={{0,1},{1,0},{2,3},{3,2},{4,5},{5,4},{6,7},{7,6},{8,9},{9,8},{10,11... | collective-permute-start | bytes 2015240 | tf_op jit(solution)/shard_map/ppermute | solution.py:48
  3.2 0.1 collective-permute-start.1
  3.3 3.5 %collective-permute-start.2 = (bf16[1,1280,128]{2,1,0:T(8,128)(2,1)S(1)}, bf16[1,1280,128]{2,1,0:T(8,128)(2,1)S(1)}, u32[]{:S(2)}, u32[]{:S(2)}) collective-permute-start(bf16[1,1280,128]{2,1,0:T(8,128)(2,1)S(1)} %get-tuple-element.31), channel_id=1, source_target_pairs={{1,2},{2,1},{5,6},{6,5},{9,10},{10,9},{13,14},{14,13},{17,18},{18,... | collective-permute-start | bytes 983048 | tf_op jit(solution)/shard_map/ppermute | solution.py:48
  6.7 2.1 %collective-permute-start.3 = (bf16[1,1280,128]{2,1,0:T(8,128)(2,1)S(1)}, bf16[1,1280,128]{2,1,0:T(8,128)(2,1)S(1)}, u32[]{:S(2)}, u32[]{:S(2)}) collective-permute-start(bf16[1,1280,128]{2,1,0:T(8,128)(2,1)S(1)} %get-tuple-element.37), channel_id=1, source_target_pairs={{1,2},{2,1},{5,6},{6,5},{9,10},{10,9},{13,14},{14,13},{17,18},{18,... | collective-permute-start | bytes 983048 | tf_op jit(solution)/shard_map/ppermute | solution.py:48
  8.8 3.5 %collective-permute-start.4 = (bf16[2,1280,128]{2,1,0:T(8,128)(2,1)S(1)}, bf16[2,1280,128]{2,1,0:T(8,128)(2,1)S(1)}, u32[]{:S(2)}, u32[]{:S(2)}) collective-permute-start(bf16[2,1280,128]{2,1,0:T(8,128)(2,1)S(1)} %get-tuple-element.42), channel_id=1, source_target_pairs={{1,2},{2,1},{5,6},{6,5},{9,10},{10,9},{13,14},{14,13},{17,18},{18,... | collective-permute-start | bytes 1966088 | tf_op jit(solution)/shard_map/ppermute | solution.py:48
  12.3 0.0 collective-permute-done.2.far_ref
  12.3 0.0 collective-permute-done.core_ref
  12.3 1.3 %compress_near.1 = (bf16[2,256,384]{2,1,0:T(8,128)(2,1)S(1)}, bf16[3,256,128]{2,1,0:T(8,128)(2,1)S(1)}) custom-call(bf16[2,1024,512]{2,1,0:T(8,128)(2,1)S(1)} %get-tuple-element.28.s_ref, bf16[2,1312,128]{2,1,0:T(8,128)(2,1)S(1)} %collective-permute-done.core_ref, bf16[1,1280,128]{2,1,0:T(8,128)(2,1)S(1)} %collective-permute-done.2.far_ref, ...), custom_call_target="tpu_custom_call" | custom-call | tf_op jit(solution)/shard_map/compress_near/pallas_call | solution.py:306
  13.6 1.3 %collective-permute-start.5 = (bf16[2,256,384]{2,1,0:T(8,128)(2,1)S(1)}, bf16[2,256,384]{2,1,0:T(8,128)(2,1)S(1)}, u32[]{:S(2)}, u32[]{:S(2)}) collective-permute-start(bf16[2,256,384]{2,1,0:T(8,128)(2,1)S(1)} %get-tuple-element.43.near_ref), channel_id=1, source_target_pairs={{0,4},{4,0},{8,12},{12,8},{16,20},{20,16},{24,28},{28,24},{1,5},{5... | collective-permute-start | bytes 1179656 | tf_op jit(solution)/shard_map/ppermute | solution.py:48
  14.9 0.0 collective-permute-done.1.core_ref
  14.9 0.3 collective-permute-done.3.far_ref
  15.2 1.1 %compress_away.1.away_ref = bf16[2,256,384]{2,1,0:T(8,128)(2,1)S(1)} custom-call(bf16[2,1024,512]{2,1,0:T(8,128)(2,1)S(1)} %get-tuple-element.28.s_ref, bf16[2,1312,128]{2,1,0:T(8,128)(2,1)S(1)} %collective-permute-done.core_ref, bf16[1,1280,128]{2,1,0:T(8,128)(2,1)S(1)} %collective-permute-done.3.far_ref, bf16[1280,256]{1,0:T(8,128)(2,1)S(1)} %get-tuple-element.32.w_ref, ...), custom_call_target="tpu_custom_call" | custom-call | tf_op jit(solution)/shard_map/compress_away/pallas_call | solution.py:306
  16.3 3.3 %collective-permute-start.6 = (bf16[2,256,384]{2,1,0:T(8,128)(2,1)S(1)}, bf16[2,256,384]{2,1,0:T(8,128)(2,1)S(1)}, u32[]{:S(2)}, u32[]{:S(2)}) collective-permute-start(bf16[2,256,384]{2,1,0:T(8,128)(2,1)S(1)} %compress_away.1.away_ref), channel_id=1, source_target_pairs={{4,8},{8,4},{12,16},{16,12},{20,24},{24,20},{5,9},{9,5},{13,17},{1... | collective-permute-start | bytes 1179656 | tf_op jit(solution)/shard_map/ppermute | solution.py:48
  19.6 0.3 %azimuth_weights.1.a_ref = bf16[3,3,512,256]{3,2,1,0:T(8,128)(2,1)S(1)} custom-call(bf16[3,2,512]{2,1,0:T(2,128)(2,1)S(1)} %get-tuple-element.40.azimuth_ref), custom_call_target="tpu_custom_call" | custom-call | tf_op jit(solution)/shard_map/azimuth_weights/pallas_call | solution.py:114
  19.9 1.0 %focus_outer.1 = (f32[2,2,256,384]{3,2,1,0:T(8,128)S(1)}, f32[2,2,256,384]{3,2,1,0:T(8,128)S(1)}) custom-call(bf16[3,3,512,256]{3,2,1,0:T(8,128)(2,1)S(1)} %azimuth_weights.1.a_ref, bf16[2,256,384]{2,1,0:T(8,128)(2,1)S(1)} %get-tuple-element.43.near_ref, bf16[2,256,384]{2,1,0:T(8,128)(2,1)S(1)} %compress_away.1.away_ref), custom_call_target="tpu_custom_call" | custom-call | tf_op jit(solution)/shard_map/focus_outer/pallas_call | solution.py:359
  20.9 1.3 %collective-permute-done.4.far_ref = bf16[2,1280,128]{2,1,0:T(8,128)(2,1)S(1)} collective-permute-done((bf16[2,1280,128]{2,1,0:T(8,128)(2,1)S(1)}, bf16[2,1280,128]{2,1,0:T(8,128)(2,1)S(1)}, u32[]{:S(2)}, u32[]{:S(2)}) %collective-permute-start.4) | collective-permute-done | bytes 655392 | tf_op jit(solution)/shard_map/ppermute | solution.py:48
  22.2 2.0 %compress_mid.1.mid_ref = bf16[2,512,384]{2,1,0:T(8,128)(2,1)S(1)} custom-call(bf16[2,1024,512]{2,1,0:T(8,128)(2,1)S(1)} %get-tuple-element.28.s_ref, bf16[2,1296,128]{2,1,0:T(8,128)(2,1)S(1)} %collective-permute-done.1.core_ref, bf16[2,1280,128]{2,1,0:T(8,128)(2,1)S(1)} %collective-permute-done.4.far_ref, bf16[1280,256]{1,0:T(8,128)(2,1)S(1)} %get-tuple-element.32.w_ref, ...), custom_call_target="tpu_custom_call" | custom-call | tf_op jit(solution)/shard_map/compress_mid/pallas_call | solution.py:306
  24.2 2.0 %focus_mid.1 = (f32[2,1024,384]{2,1,0:T(8,128)}, f32[2,2,256,384]{3,2,1,0:T(8,128)S(1)}) custom-call(bf16[3,3,512,256]{3,2,1,0:T(8,128)(2,1)S(1)} %azimuth_weights.1.a_ref, bf16[2,512,384]{2,1,0:T(8,128)(2,1)S(1)} %compress_mid.1.mid_ref, f32[2,2,256,384]{3,2,1,0:T(8,128)S(1)} %get-tuple-element.47.part_ref, ...), custom_call_target="tpu_custom_call" | custom-call | tf_op jit(solution)/shard_map/focus_mid/pallas_call | solution.py:395
  26.2 1.8 %collective-permute-done.5.halo_ref = bf16[2,256,384]{2,1,0:T(8,128)(2,1)S(1)} collective-permute-done((bf16[2,256,384]{2,1,0:T(8,128)(2,1)S(1)}, bf16[2,256,384]{2,1,0:T(8,128)(2,1)S(1)}, u32[]{:S(2)}, u32[]{:S(2)}) %collective-permute-start.5) | collective-permute-done | bytes 393248 | tf_op jit(solution)/shard_map/ppermute | solution.py:48
  28.1 0.4 %near_end.1.near_ref = f32[2,256,384]{2,1,0:T(8,128)S(1)} custom-call(bf16[3,3,512,256]{3,2,1,0:T(8,128)(2,1)S(1)} %azimuth_weights.1.a_ref, f32[2,2,256,384]{3,2,1,0:T(8,128)S(1)} %get-tuple-element.49.part_ref, bf16[2,256,384]{2,1,0:T(8,128)(2,1)S(1)} %collective-permute-done.5.halo_ref), custom_call_target="tpu_custom_call" | custom-call | tf_op jit(solution)/shard_map/near_end/pallas_call | solution.py:421
  28.5 0.0 collective-permute-done.6.halo_ref
  28.5 1.2 %ends.1 = f32[2,1024,384]{2,1,0:T(8,128)} custom-call(bf16[3,3,512,256]{3,2,1,0:T(8,128)(2,1)S(1)} %azimuth_weights.1.a_ref, f32[2,2,256,384]{3,2,1,0:T(8,128)S(1)} %get-tuple-element.49.part_ref, f32[2,256,384]{2,1,0:T(8,128)S(1)} %near_end.1.near_ref, bf16[2,256,384]{2,1,0:T(8,128)(2,1)S(1)} %collective-permute-done.6.halo_ref, ...), custom_call_target="tpu_custom_call", output_to_operand_aliasing={{}: (4, {})} | custom-call | tf_op jit(solution)/shard_map/ends/pallas_call | solution.py:468
Async XLA Ops:
  2.5 9.9 %collective-permute-start = (bf16[2,1312,128]{2,1,0:T(8,128)(2,1)S(1)}, bf16[2,1312,128]{2,1,0:T(8,128)(2,1)S(1)}, u32[]{:S(2)}, u32[]{:S(2)}) collective-permute-start(bf16[2,1312,128]{2,1,0:T(8,128)(2,1)S(1)} %get-tuple-element.29), channel_id=1, source_target_pairs={{0,1},{1,0},{2,3},{3,2},{4,5},{5,4},{6,7},{7,6},{8,9},{9,8},{10,11... | collective-permute-start | bytes 2015240 | tf_op jit(solution)/shard_map/ppermute | solution.py:48
  3.2 11.7 %collective-permute-start.1 = (bf16[2,1296,128]{2,1,0:T(8,128)(2,1)S(1)}, bf16[2,1296,128]{2,1,0:T(8,128)(2,1)S(1)}, u32[]{:S(2)}, u32[]{:S(2)}) collective-permute-start(bf16[2,1296,128]{2,1,0:T(8,128)(2,1)S(1)} %get-tuple-element.30), channel_id=1, source_target_pairs={{0,1},{1,0},{2,3},{3,2},{4,5},{5,4},{6,7},{7,6},{8,9},{9,8},{10,11... | collective-permute-start | bytes 1990664 | tf_op jit(solution)/shard_map/ppermute | solution.py:48
  3.3 9.0 %collective-permute-start.2 = (bf16[1,1280,128]{2,1,0:T(8,128)(2,1)S(1)}, bf16[1,1280,128]{2,1,0:T(8,128)(2,1)S(1)}, u32[]{:S(2)}, u32[]{:S(2)}) collective-permute-start(bf16[1,1280,128]{2,1,0:T(8,128)(2,1)S(1)} %get-tuple-element.31), channel_id=1, source_target_pairs={{1,2},{2,1},{5,6},{6,5},{9,10},{10,9},{13,14},{14,13},{17,18},{18,... | collective-permute-start | bytes 983048 | tf_op jit(solution)/shard_map/ppermute | solution.py:48
  6.7 8.4 %collective-permute-start.3 = (bf16[1,1280,128]{2,1,0:T(8,128)(2,1)S(1)}, bf16[1,1280,128]{2,1,0:T(8,128)(2,1)S(1)}, u32[]{:S(2)}, u32[]{:S(2)}) collective-permute-start(bf16[1,1280,128]{2,1,0:T(8,128)(2,1)S(1)} %get-tuple-element.37), channel_id=1, source_target_pairs={{1,2},{2,1},{5,6},{6,5},{9,10},{10,9},{13,14},{14,13},{17,18},{18,... | collective-permute-start | bytes 983048 | tf_op jit(solution)/shard_map/ppermute | solution.py:48
  8.8 13.3 %collective-permute-start.4 = (bf16[2,1280,128]{2,1,0:T(8,128)(2,1)S(1)}, bf16[2,1280,128]{2,1,0:T(8,128)(2,1)S(1)}, u32[]{:S(2)}, u32[]{:S(2)}) collective-permute-start(bf16[2,1280,128]{2,1,0:T(8,128)(2,1)S(1)} %get-tuple-element.42), channel_id=1, source_target_pairs={{1,2},{2,1},{5,6},{6,5},{9,10},{10,9},{13,14},{14,13},{17,18},{18,... | collective-permute-start | bytes 1966088 | tf_op jit(solution)/shard_map/ppermute | solution.py:48
  13.6 14.5 %collective-permute-start.5 = (bf16[2,256,384]{2,1,0:T(8,128)(2,1)S(1)}, bf16[2,256,384]{2,1,0:T(8,128)(2,1)S(1)}, u32[]{:S(2)}, u32[]{:S(2)}) collective-permute-start(bf16[2,256,384]{2,1,0:T(8,128)(2,1)S(1)} %get-tuple-element.43.near_ref), channel_id=1, source_target_pairs={{0,4},{4,0},{8,12},{12,8},{16,20},{20,16},{24,28},{28,24},{1,5},{5... | collective-permute-start | bytes 1179656 | tf_op jit(solution)/shard_map/ppermute | solution.py:48
  16.3 12.2 %collective-permute-start.6 = (bf16[2,256,384]{2,1,0:T(8,128)(2,1)S(1)}, bf16[2,256,384]{2,1,0:T(8,128)(2,1)S(1)}, u32[]{:S(2)}, u32[]{:S(2)}) collective-permute-start(bf16[2,256,384]{2,1,0:T(8,128)(2,1)S(1)} %compress_away.1.away_ref), channel_id=1, source_target_pairs={{4,8},{8,4},{12,16},{16,12},{20,24},{24,20},{5,9},{9,5},{13,17},{1... | collective-permute-start | bytes 1179656 | tf_op jit(solution)/shard_map/ppermute | solution.py:48

commit v3 on v1

--- a/solution.py
+++ b/solution.py
@@ -125,30 +125,22 @@
     return slice(t * LANES, (t + 1) * LANES)
 
 
-def edge_chunk(x_ref, s_ref, start, targets):
+def write_edge(x_ref, start, out_ref, chunk, side):
     picked = pl.ds(start, CHUNK)
     half = CHUNK // 2
-    low, low_half = low_lanes(CHUNK), low_lanes(half)
-    count = x_ref.shape[2] // LANES
+    low = low_lanes(half)
+    last = x_ref.shape[2] // LANES - 1
     for part in range(2):
-        cells = [x_ref[part, picked, tile_of(t)] for t in range(count)]
-        rolled = [lane_roll(c) for c in cells]
-        tiles = [rolled[0]]
-        tiles += [jnp.where(low, rolled[t], rolled[t + 1]) for t in range(count - 1)]
-        tiles += [rolled[-1]]
-        for t, tile in enumerate(tiles):
-            s_ref[part, picked, tile_of(t)] = tile
-        for out_ref, chunk, side in targets:
-            inner = (1, 2) if side == 0 else (count - 2, count - 1)
-            for i, t in enumerate(inner):
-                at = (2 * part + i) * CHUNK
-                out_ref[chunk, at : at + CHUNK, :] = tiles[t]
-            at = 4 * CHUNK + part * half
-            if side == 0:
-                packed = jnp.where(low_half, cells[0][:half], rolled[0][half:])
-            else:
-                packed = jnp.where(low_half, rolled[-1][:half], cells[-1][half:])
-            out_ref[chunk, at : at + half, :] = packed
+        for i, t in enumerate((0, 1) if side == 0 else (last - 1, last)):
+            at = (2 * part + i) * CHUNK
+            out_ref[chunk, at : at + CHUNK, :] = x_ref[part, picked, tile_of(t)]
+        cells = x_ref[part, picked, tile_of(2 if side == 0 else last - 2)]
+        top, bottom = cells[:half], cells[half:]
+        at = 4 * CHUNK + part * half
+        if side == 0:
+            out_ref[chunk, at : at + half, :] = jnp.where(low, top, lane_roll(bottom))
+        else:
+            out_ref[chunk, at : at + half, :] = jnp.where(low, lane_roll(top), bottom)
 
 
 def near_away_rows(rows):
@@ -161,8 +153,8 @@
 
 def edges_kernel(
     x_hbm, range_hbm, taps_hbm, shift_hbm, azimuth_hbm,
-    s_ref, far_near_ref, far_away_ref, far_mid_ref, core_outer_ref, core_mid_ref,
-    w_ref, taps_ref, splat_ref, azimuth_ref, x_ref, range_ref, shift_ref, sems,
+    x_ref, far_near_ref, far_away_ref, far_mid_ref, core_outer_ref, core_mid_ref,
+    w_ref, taps_ref, splat_ref, azimuth_ref, range_ref, shift_ref, sems,
 ):
     rows = x_ref.shape[1]
     near, away = near_away_rows(rows)
@@ -197,7 +189,8 @@
             copies[small + i].wait()
             far = [(far_near_ref, 0), (far_away_ref, 0)][i] if i < 2 else (far_mid_ref, i - 2)
             core = (core_outer_ref, i) if i < 2 else (core_mid_ref, i - 2)
-            edge_chunk(x_ref, s_ref, start, [core + (1 - odd,), far + (odd,)])
+            write_edge(x_ref, start, *core, 1 - odd)
+            write_edge(x_ref, start, *far, odd)
 
     by_parity("rg", body)
 
@@ -209,7 +202,7 @@
     args = (raw, range_chirp, migration_taps, block_shift, azimuth_chirp)
     return pl.pallas_call(
         edges_kernel,
-        out_shape=(jax.ShapeDtypeStruct(raw.shape[:2] + (raw.shape[2] + LANES,), BF16),)
+        out_shape=(jax.ShapeDtypeStruct(raw.shape, BF16),)
         + tuple(
             jax.ShapeDtypeStruct((n, 5 * CHUNK + extra, LANES), BF16)
             for n, extra in ((1, 0), (1, 0), (chunks - 2, 0), (2, 2 * PAD), (chunks - 2, PAD))
@@ -223,7 +216,6 @@
         in_specs=[pl.BlockSpec(memory_space=pltpu.HBM)] * len(args),
         out_specs=(pl.BlockSpec(memory_space=pltpu.VMEM),) * 10,
         scratch_shapes=[
-            pltpu.VMEM(raw.shape, BF16),
             pltpu.VMEM(range_chirp.shape, BF16),
             pltpu.SMEM(block_shift.shape, jnp.int32),
             pltpu.SemaphoreType.DMA((chunks + len(args) - 1,)),
@@ -233,27 +225,27 @@
     )(*(in_hbm(x) for x in args))
 
 
-def window_tiles(s_ref, start, left, right, part):
+def window_tiles(x_ref, start, left, right, part):
     half = CHUNK // 2
     low = low_lanes(CHUNK)
     picked = pl.ds(start, CHUNK)
-    last = s_ref.shape[2] // LANES - 1
-    inner = slice(4 * CHUNK + part * half, 4 * CHUNK + (part + 1) * half)
-
-    def full(halo):
-        ref, chunk = halo
-        return [
-            ref[chunk, (2 * part + i) * CHUNK : (2 * part + i + 1) * CHUNK, :] for i in range(2)
-        ]
-
-    packed = left[0][left[1], inner, :]
-    halo = jnp.concatenate([packed, lane_roll(packed)], axis=0)
-    first = jnp.where(low, halo, s_ref[part, picked, tile_of(0)])
-    packed = right[0][right[1], inner, :]
-    halo = jnp.concatenate([lane_roll(packed), packed], axis=0)
-    final = jnp.where(low, s_ref[part, picked, tile_of(last)], halo)
-    own = [s_ref[part, picked, tile_of(t)] for t in range(1, last)]
-    return full(left) + [first] + own + [final] + full(right)
+
+    def halo(edge):
+        ref, chunk = edge
+        at = 4 * CHUNK + part * half
+        tiles = [ref[chunk, (2 * part + i) * CHUNK : (2 * part + i + 1) * CHUNK, :] for i in (0, 1)]
+        return tiles, ref[chunk, at : at + half, :]
+
+    before, first = halo(left)
+    after, final = halo(right)
+    own = [x_ref[part, picked, tile_of(t)] for t in range(x_ref.shape[2] // LANES)]
+    rolled = [lane_roll(t) for t in before + own + after]
+    rolled = (
+        [jnp.concatenate([first, lane_roll(first)], axis=0)]
+        + rolled
+        + [jnp.concatenate([lane_roll(final), final], axis=0)]
+    )
+    return [jnp.where(low, rolled[i], rolled[i + 1]) for i in range(len(rolled) - 1)]
 
 
 def compress_chunk(s_ref, start, left, right, w_ref, m_ref, out_ref, out_start, c_ref):
@@ -296,10 +288,10 @@
     by_parity("rg", body)
 
 
-def compress(which, shifted, core, far, w, *bands):
-    rows, cells = shifted.shape[1], shifted.shape[2] - LANES
+def compress(which, echo, core, far, w, *bands):
+    rows, cells = echo.shape[1], echo.shape[2]
     count = rows // CHUNK - 2 if which == "mid" else 1
-    args = (shifted, core, far, w) + bands
+    args = (echo, core, far, w) + bands
     out = (jax.ShapeDtypeStruct((2, count * CHUNK, cells), BF16),)
     if which == "near":
         out += (jax.ShapeDtypeStruct((cells // LANES, 2 * LANES, LANES), BF16),)
@@ -460,7 +452,7 @@
 
 
 def per_device(raw_echo, range_chirp, migration_taps, block_shift, azimuth_chirp):
-    shifted, far_near, far_away, far_mid, core_outer, core_mid, w, taps, splat, azimuth_chirp = range_edges(
+    echo, far_near, far_away, far_mid, core_outer, core_mid, w, taps, splat, azimuth_chirp = range_edges(
         raw_echo, range_chirp, migration_taps, block_shift, azimuth_chirp
     )
     core_outer = swap(core_outer, "rg", 0)
@@ -468,16 +460,16 @@
     far_near = swap(far_near, "rg", 1)
     far_away = swap(far_away, "rg", 1)
     far_mid = swap(far_mid, "rg", 1)
-    near, m = compress("near", shifted, core_outer, far_near, w, taps, splat)
+    near, m = compress("near", echo, core_outer, far_near, w, taps, splat)
     near_halo = swap(near, "az", 0)
     core_outer, core_mid, near = lax.optimization_barrier((core_outer, core_mid, near))
-    away = compress("away", shifted, core_outer, far_away, w, m)
+    away = compress("away", echo, core_outer, far_away, w, m)
     away_halo = swap(away, "az", 1)
     away, azimuth_chirp = lax.optimization_barrier((away, azimuth_chirp))
     a = azimuth_weights(azimuth_chirp)
     part, mid_part = focus_outer(a, near, away, raw_echo.shape[1] // CHUNK - 2)
     far_mid, part = lax.optimization_barrier((far_mid, part))
-    mid = compress("mid", shifted, core_mid, far_mid, w, m)
+    mid = compress("mid", echo, core_mid, far_mid, w, m)
     image, part = focus_mid(a, mid, part, mid_part)
     return ends(a, part, near_end(a, part, near_halo), away_halo, image)
 

time: 29.7 us -> 29.6 us (level)
  transfers between devices with their start and end apart: 7 -> 7, of which waited for: 3 -> 3; matrix products, arithmetic and copies ran while one was open for 0% -> 0% of each run, Pallas kernels for 27% -> 28%
where the time goes in v3:
time: 29.6 us; the launch traced here: 29.4 us
  starting transfers between devices  14.4 us (49%)
  Pallas kernels  11.4 us (39%)
  waiting for transfers between devices  3.3 us (11%)
    ppermute x7, starting transfers between devices, swap(): return lax.ppermute(x, axis, swap_pairs(lax.axis_size(axis), first))  14.4 us
    pallas_call x3, Pallas kernels, compress(): pl.pallas_call(functools.partial(compress_kernel, which), out_shape=out,...  4.61 us
    ppermute x7, waiting for transfers between devices, swap(): return lax.ppermute(x, axis, swap_pairs(lax.axis_size(axis), first))  3.3 us
    pallas_call x1, Pallas kernels, focus_mid(): pl.pallas_call(focus_mid_kernel, out_shape=(jax.ShapeDtypeStruct((2, (mid...  2.02 us
    pallas_call x1, Pallas kernels, range_edges(): pl.pallas_call(edges_kernel, out_shape=(jax.ShapeDtypeStruct(raw.shape, B...  1.82 us
    pallas_call x1, Pallas kernels, ends(): pl.pallas_call(ends_kernel, out_shape=jax.ShapeDtypeStruct(image.shape, F...  1.29 us
    pallas_call x1, Pallas kernels, focus_outer(): pl.pallas_call(focus_outer_kernel, out_shape=(jax.ShapeDtypeStruct((2, 2,...  1 us
  transfers between devices with their start and end apart: 7, of which 3 were waited for; matrix products, arithmetic and copies ran while one was open for 0% of the time, Pallas kernels for 28%

profile of v3, /device:TPU:17, one launch (start us, length us, event | category | flops | bytes accessed | tf_op | source)
XLA Modules:
  0.0 29.4 jit_solution(13011928757382542923)
XLA Ops:
  0.0 1.8 %range_edges.1 = (bf16[2,1024,384]{2,1,0:T(8,128)(2,1)S(1)}, bf16[1,1280,128]{2,1,0:T(8,128)(2,1)S(1)}, bf16[1,1280,128]{2,1,0:T(8,128)(2,1)S(1)}, bf16[2,1280,1...) custom-call(bf16[2,1024,384]{2,1,0:T(8,128)(2,1)} %x_hbm.1, ...), custom_call_target="tpu_custom_call" | custom-call | tf_op jit(solution)/shard_map/range_edges/pallas_call | solution.py:203
  1.8 0.7 %collective-permute-start = (bf16[2,1312,128]{2,1,0:T(8,128)(2,1)S(1)}, bf16[2,1312,128]{2,1,0:T(8,128)(2,1)S(1)}, u32[]{:S(2)}, u32[]{:S(2)}) collective-permute-start(bf16[2,1312,128]{2,1,0:T(8,128)(2,1)S(1)} %get-tuple-element.29), channel_id=1, source_target_pairs={{0,1},{1,0},{2,3},{3,2},{4,5},{5,4},{6,7},{7,6},{8,9},{9,8},{10,11... | collective-permute-start | bytes 2015240 | tf_op jit(solution)/shard_map/ppermute | solution.py:48
  2.6 0.1 collective-permute-start.1
  2.6 3.5 %collective-permute-start.2 = (bf16[1,1280,128]{2,1,0:T(8,128)(2,1)S(1)}, bf16[1,1280,128]{2,1,0:T(8,128)(2,1)S(1)}, u32[]{:S(2)}, u32[]{:S(2)}) collective-permute-start(bf16[1,1280,128]{2,1,0:T(8,128)(2,1)S(1)} %get-tuple-element.31), channel_id=1, source_target_pairs={{1,2},{2,1},{5,6},{6,5},{9,10},{10,9},{13,14},{14,13},{17,18},{18,... | collective-permute-start | bytes 983048 | tf_op jit(solution)/shard_map/ppermute | solution.py:48
  6.1 2.1 %collective-permute-start.3 = (bf16[1,1280,128]{2,1,0:T(8,128)(2,1)S(1)}, bf16[1,1280,128]{2,1,0:T(8,128)(2,1)S(1)}, u32[]{:S(2)}, u32[]{:S(2)}) collective-permute-start(bf16[1,1280,128]{2,1,0:T(8,128)(2,1)S(1)} %get-tuple-element.37), channel_id=1, source_target_pairs={{1,2},{2,1},{5,6},{6,5},{9,10},{10,9},{13,14},{14,13},{17,18},{18,... | collective-permute-start | bytes 983048 | tf_op jit(solution)/shard_map/ppermute | solution.py:48
  8.2 3.5 %collective-permute-start.4 = (bf16[2,1280,128]{2,1,0:T(8,128)(2,1)S(1)}, bf16[2,1280,128]{2,1,0:T(8,128)(2,1)S(1)}, u32[]{:S(2)}, u32[]{:S(2)}) collective-permute-start(bf16[2,1280,128]{2,1,0:T(8,128)(2,1)S(1)} %get-tuple-element.42), channel_id=1, source_target_pairs={{1,2},{2,1},{5,6},{6,5},{9,10},{10,9},{13,14},{14,13},{17,18},{18,... | collective-permute-start | bytes 1966088 | tf_op jit(solution)/shard_map/ppermute | solution.py:48
  11.7 0.0 collective-permute-done.2.far_ref
  11.7 0.0 collective-permute-done.core_ref
  11.7 1.3 %compress_near.1 = (bf16[2,256,384]{2,1,0:T(8,128)(2,1)S(1)}, bf16[3,256,128]{2,1,0:T(8,128)(2,1)S(1)}) custom-call(bf16[2,1024,384]{2,1,0:T(8,128)(2,1)S(1)} %get-tuple-element.28.s_ref, bf16[2,1312,128]{2,1,0:T(8,128)(2,1)S(1)} %collective-permute-done.core_ref, bf16[1,1280,128]{2,1,0:T(8,128)(2,1)S(1)} %collective-permute-done.2.far_ref, ...), custom_call_target="tpu_custom_call" | custom-call | tf_op jit(solution)/shard_map/compress_near/pallas_call | solution.py:298
  13.0 1.3 %collective-permute-start.5 = (bf16[2,256,384]{2,1,0:T(8,128)(2,1)S(1)}, bf16[2,256,384]{2,1,0:T(8,128)(2,1)S(1)}, u32[]{:S(2)}, u32[]{:S(2)}) collective-permute-start(bf16[2,256,384]{2,1,0:T(8,128)(2,1)S(1)} %get-tuple-element.43.near_ref), channel_id=1, source_target_pairs={{0,4},{4,0},{8,12},{12,8},{16,20},{20,16},{24,28},{28,24},{1,5},{5... | collective-permute-start | bytes 1179656 | tf_op jit(solution)/shard_map/ppermute | solution.py:48
  14.3 0.0 collective-permute-done.1.core_ref
  14.3 0.2 collective-permute-done.3.far_ref
  14.5 1.2 %compress_away.1.away_ref = bf16[2,256,384]{2,1,0:T(8,128)(2,1)S(1)} custom-call(bf16[2,1024,384]{2,1,0:T(8,128)(2,1)S(1)} %get-tuple-element.28.s_ref, bf16[2,1312,128]{2,1,0:T(8,128)(2,1)S(1)} %collective-permute-done.core_ref, bf16[1,1280,128]{2,1,0:T(8,128)(2,1)S(1)} %collective-permute-done.3.far_ref, bf16[1280,256]{1,0:T(8,128)(2,1)S(1)} %get-tuple-element.32.w_ref, ...), custom_call_target="tpu_custom_call" | custom-call | tf_op jit(solution)/shard_map/compress_away/pallas_call | solution.py:298
  15.7 3.3 %collective-permute-start.6 = (bf16[2,256,384]{2,1,0:T(8,128)(2,1)S(1)}, bf16[2,256,384]{2,1,0:T(8,128)(2,1)S(1)}, u32[]{:S(2)}, u32[]{:S(2)}) collective-permute-start(bf16[2,256,384]{2,1,0:T(8,128)(2,1)S(1)} %compress_away.1.away_ref), channel_id=1, source_target_pairs={{4,8},{8,4},{12,16},{16,12},{20,24},{24,20},{5,9},{9,5},{13,17},{1... | collective-permute-start | bytes 1179656 | tf_op jit(solution)/shard_map/ppermute | solution.py:48
  19.0 0.3 %azimuth_weights.1.a_ref = bf16[3,3,512,256]{3,2,1,0:T(8,128)(2,1)S(1)} custom-call(bf16[3,2,512]{2,1,0:T(2,128)(2,1)S(1)} %get-tuple-element.40.azimuth_ref), custom_call_target="tpu_custom_call" | custom-call | tf_op jit(solution)/shard_map/azimuth_weights/pallas_call | solution.py:114
  19.3 1.0 %focus_outer.1 = (f32[2,2,256,384]{3,2,1,0:T(8,128)S(1)}, f32[2,2,256,384]{3,2,1,0:T(8,128)S(1)}) custom-call(bf16[3,3,512,256]{3,2,1,0:T(8,128)(2,1)S(1)} %azimuth_weights.1.a_ref, bf16[2,256,384]{2,1,0:T(8,128)(2,1)S(1)} %get-tuple-element.43.near_ref, bf16[2,256,384]{2,1,0:T(8,128)(2,1)S(1)} %compress_away.1.away_ref), custom_call_target="tpu_custom_call" | custom-call | tf_op jit(solution)/shard_map/focus_outer/pallas_call | solution.py:351
  20.3 1.2 %collective-permute-done.4.far_ref = bf16[2,1280,128]{2,1,0:T(8,128)(2,1)S(1)} collective-permute-done((bf16[2,1280,128]{2,1,0:T(8,128)(2,1)S(1)}, bf16[2,1280,128]{2,1,0:T(8,128)(2,1)S(1)}, u32[]{:S(2)}, u32[]{:S(2)}) %collective-permute-start.4) | collective-permute-done | bytes 655392 | tf_op jit(solution)/shard_map/ppermute | solution.py:48
  21.6 2.1 %compress_mid.1.mid_ref = bf16[2,512,384]{2,1,0:T(8,128)(2,1)S(1)} custom-call(bf16[2,1024,384]{2,1,0:T(8,128)(2,1)S(1)} %get-tuple-element.28.s_ref, bf16[2,1296,128]{2,1,0:T(8,128)(2,1)S(1)} %collective-permute-done.1.core_ref, bf16[2,1280,128]{2,1,0:T(8,128)(2,1)S(1)} %collective-permute-done.4.far_ref, bf16[1280,256]{1,0:T(8,128)(2,1)S(1)} %get-tuple-element.32.w_ref, ...), custom_call_target="tpu_custom_call" | custom-call | tf_op jit(solution)/shard_map/compress_mid/pallas_call | solution.py:298
  23.7 2.0 %focus_mid.1 = (f32[2,1024,384]{2,1,0:T(8,128)}, f32[2,2,256,384]{3,2,1,0:T(8,128)S(1)}) custom-call(bf16[3,3,512,256]{3,2,1,0:T(8,128)(2,1)S(1)} %azimuth_weights.1.a_ref, bf16[2,512,384]{2,1,0:T(8,128)(2,1)S(1)} %compress_mid.1.mid_ref, f32[2,2,256,384]{3,2,1,0:T(8,128)S(1)} %get-tuple-element.47.part_ref, ...), custom_call_target="tpu_custom_call" | custom-call | tf_op jit(solution)/shard_map/focus_mid/pallas_call | solution.py:387
  25.7 1.8 %collective-permute-done.5.halo_ref = bf16[2,256,384]{2,1,0:T(8,128)(2,1)S(1)} collective-permute-done((bf16[2,256,384]{2,1,0:T(8,128)(2,1)S(1)}, bf16[2,256,384]{2,1,0:T(8,128)(2,1)S(1)}, u32[]{:S(2)}, u32[]{:S(2)}) %collective-permute-start.5) | collective-permute-done | bytes 393248 | tf_op jit(solution)/shard_map/ppermute | solution.py:48
  27.5 0.4 %near_end.1.near_ref = f32[2,256,384]{2,1,0:T(8,128)S(1)} custom-call(bf16[3,3,512,256]{3,2,1,0:T(8,128)(2,1)S(1)} %azimuth_weights.1.a_ref, f32[2,2,256,384]{3,2,1,0:T(8,128)S(1)} %get-tuple-element.49.part_ref, bf16[2,256,384]{2,1,0:T(8,128)(2,1)S(1)} %collective-permute-done.5.halo_ref), custom_call_target="tpu_custom_call" | custom-call | tf_op jit(solution)/shard_map/near_end/pallas_call | solution.py:413
  27.9 0.0 collective-permute-done.6.halo_ref
  27.9 1.3 %ends.1 = f32[2,1024,384]{2,1,0:T(8,128)} custom-call(bf16[3,3,512,256]{3,2,1,0:T(8,128)(2,1)S(1)} %azimuth_weights.1.a_ref, f32[2,2,256,384]{3,2,1,0:T(8,128)S(1)} %get-tuple-element.49.part_ref, f32[2,256,384]{2,1,0:T(8,128)S(1)} %near_end.1.near_ref, bf16[2,256,384]{2,1,0:T(8,128)(2,1)S(1)} %collective-permute-done.6.halo_ref, ...), custom_call_target="tpu_custom_call", output_to_operand_aliasing={{}: (4, {})} | custom-call | tf_op jit(solution)/shard_map/ends/pallas_call | solution.py:441
Async XLA Ops:
  1.8 9.9 %collective-permute-start = (bf16[2,1312,128]{2,1,0:T(8,128)(2,1)S(1)}, bf16[2,1312,128]{2,1,0:T(8,128)(2,1)S(1)}, u32[]{:S(2)}, u32[]{:S(2)}) collective-permute-start(bf16[2,1312,128]{2,1,0:T(8,128)(2,1)S(1)} %get-tuple-element.29), channel_id=1, source_target_pairs={{0,1},{1,0},{2,3},{3,2},{4,5},{5,4},{6,7},{7,6},{8,9},{9,8},{10,11... | collective-permute-start | bytes 2015240 | tf_op jit(solution)/shard_map/ppermute | solution.py:48
  2.6 11.7 %collective-permute-start.1 = (bf16[2,1296,128]{2,1,0:T(8,128)(2,1)S(1)}, bf16[2,1296,128]{2,1,0:T(8,128)(2,1)S(1)}, u32[]{:S(2)}, u32[]{:S(2)}) collective-permute-start(bf16[2,1296,128]{2,1,0:T(8,128)(2,1)S(1)} %get-tuple-element.30), channel_id=1, source_target_pairs={{0,1},{1,0},{2,3},{3,2},{4,5},{5,4},{6,7},{7,6},{8,9},{9,8},{10,11... | collective-permute-start | bytes 1990664 | tf_op jit(solution)/shard_map/ppermute | solution.py:48
  2.6 9.0 %collective-permute-start.2 = (bf16[1,1280,128]{2,1,0:T(8,128)(2,1)S(1)}, bf16[1,1280,128]{2,1,0:T(8,128)(2,1)S(1)}, u32[]{:S(2)}, u32[]{:S(2)}) collective-permute-start(bf16[1,1280,128]{2,1,0:T(8,128)(2,1)S(1)} %get-tuple-element.31), channel_id=1, source_target_pairs={{1,2},{2,1},{5,6},{6,5},{9,10},{10,9},{13,14},{14,13},{17,18},{18,... | collective-permute-start | bytes 983048 | tf_op jit(solution)/shard_map/ppermute | solution.py:48
  6.1 8.4 %collective-permute-start.3 = (bf16[1,1280,128]{2,1,0:T(8,128)(2,1)S(1)}, bf16[1,1280,128]{2,1,0:T(8,128)(2,1)S(1)}, u32[]{:S(2)}, u32[]{:S(2)}) collective-permute-start(bf16[1,1280,128]{2,1,0:T(8,128)(2,1)S(1)} %get-tuple-element.37), channel_id=1, source_target_pairs={{1,2},{2,1},{5,6},{6,5},{9,10},{10,9},{13,14},{14,13},{17,18},{18,... | collective-permute-start | bytes 983048 | tf_op jit(solution)/shard_map/ppermute | solution.py:48
  8.2 13.3 %collective-permute-start.4 = (bf16[2,1280,128]{2,1,0:T(8,128)(2,1)S(1)}, bf16[2,1280,128]{2,1,0:T(8,128)(2,1)S(1)}, u32[]{:S(2)}, u32[]{:S(2)}) collective-permute-start(bf16[2,1280,128]{2,1,0:T(8,128)(2,1)S(1)} %get-tuple-element.42), channel_id=1, source_target_pairs={{1,2},{2,1},{5,6},{6,5},{9,10},{10,9},{13,14},{14,13},{17,18},{18,... | collective-permute-start | bytes 1966088 | tf_op jit(solution)/shard_map/ppermute | solution.py:48
  13.0 14.5 %collective-permute-start.5 = (bf16[2,256,384]{2,1,0:T(8,128)(2,1)S(1)}, bf16[2,256,384]{2,1,0:T(8,128)(2,1)S(1)}, u32[]{:S(2)}, u32[]{:S(2)}) collective-permute-start(bf16[2,256,384]{2,1,0:T(8,128)(2,1)S(1)} %get-tuple-element.43.near_ref), channel_id=1, source_target_pairs={{0,4},{4,0},{8,12},{12,8},{16,20},{20,16},{24,28},{28,24},{1,5},{5... | collective-permute-start | bytes 1179656 | tf_op jit(solution)/shard_map/ppermute | solution.py:48
  15.7 12.2 %collective-permute-start.6 = (bf16[2,256,384]{2,1,0:T(8,128)(2,1)S(1)}, bf16[2,256,384]{2,1,0:T(8,128)(2,1)S(1)}, u32[]{:S(2)}, u32[]{:S(2)}) collective-permute-start(bf16[2,256,384]{2,1,0:T(8,128)(2,1)S(1)} %compress_away.1.away_ref), channel_id=1, source_target_pairs={{4,8},{8,4},{12,16},{16,12},{20,24},{24,20},{5,9},{9,5},{13,17},{1... | collective-permute-start | bytes 1179656 | tf_op jit(solution)/shard_map/ppermute | solution.py:48

commit v4 on v3

--- a/solution.py
+++ b/solution.py
@@ -165,7 +165,6 @@
         (shift_hbm, shift_ref),
         (azimuth_hbm, azimuth_ref),
     ]
-    small = len(moves)
     for start in starts:
         picked = pl.ds(start, CHUNK)
         moves.append((x_hbm.at[:, picked, :], x_ref.at[:, picked, :]))
@@ -175,18 +174,17 @@
     ]
     for copy in copies:
         copy.start()
-    for copy in copies[:small]:
+    for copy in copies:
         copy.wait()
-    for ref in (core_outer_ref, core_mid_ref):
-        extra = ref.shape[1] - 5 * CHUNK
-        ref[:, 5 * CHUNK :, :] = jnp.zeros((ref.shape[0], extra, LANES), BF16)
-    range_toeplitz(range_ref, w_ref)
-    for b in range(splat_ref.shape[0]):
-        splat_ref[b] = jnp.full(splat_ref.shape[1:], shift_ref[b], jnp.int32)
 
     def body(odd):
+        for ref in (core_outer_ref, core_mid_ref):
+            extra = ref.shape[1] - 5 * CHUNK
+            ref[:, 5 * CHUNK :, :] = jnp.zeros((ref.shape[0], extra, LANES), BF16)
+        for b in range(splat_ref.shape[0]):
+            splat_ref[b] = jnp.full(splat_ref.shape[1:], shift_ref[b], jnp.int32)
+        range_toeplitz(range_ref, w_ref)
         for i, start in enumerate(starts):
-            copies[small + i].wait()
             far = [(far_near_ref, 0), (far_away_ref, 0)][i] if i < 2 else (far_mid_ref, i - 2)
             core = (core_outer_ref, i) if i < 2 else (core_mid_ref, i - 2)
             write_edge(x_ref, start, *core, 1 - odd)

time: 29.6 us -> 29.9 us (1.010)
  Pallas kernels: 11.4 us -> 11.8 us
    pallas_call x1, Pallas kernels: 1.82 us -> 2.15 us  [range_edges(): pl.pallas_call(edges_kernel, out_shape=(jax.ShapeDtypeStruct(raw.shape, B...]
where the time goes in v4:
time: 29.9 us; the launch traced here: 29.7 us
  starting transfers between devices  14.4 us (48%)
  Pallas kernels  11.8 us (39%)
  waiting for transfers between devices  3.3 us (11%)
    ppermute x7, starting transfers between devices, swap(): return lax.ppermute(x, axis, swap_pairs(lax.axis_size(axis), first))  14.4 us
    pallas_call x3, Pallas kernels, compress(): pl.pallas_call(functools.partial(compress_kernel, which), out_shape=out,...  4.61 us
    ppermute x7, waiting for transfers between devices, swap(): return lax.ppermute(x, axis, swap_pairs(lax.axis_size(axis), first))  3.3 us
    pallas_call x1, Pallas kernels, range_edges(): pl.pallas_call(edges_kernel, out_shape=(jax.ShapeDtypeStruct(raw.shape, B...  2.15 us
    pallas_call x1, Pallas kernels, focus_mid(): pl.pallas_call(focus_mid_kernel, out_shape=(jax.ShapeDtypeStruct((2, (mid...  2.02 us
    pallas_call x1, Pallas kernels, ends(): pl.pallas_call(ends_kernel, out_shape=jax.ShapeDtypeStruct(image.shape, F...  1.29 us
    pallas_call x1, Pallas kernels, focus_outer(): pl.pallas_call(focus_outer_kernel, out_shape=(jax.ShapeDtypeStruct((2, 2,...  1 us
  transfers between devices with their start and end apart: 7, of which 3 were waited for; matrix products, arithmetic and copies ran while one was open for 0% of the time, Pallas kernels for 28%

profile of v4, /device:TPU:17, one launch (start us, length us, event | category | flops | bytes accessed | tf_op | source)
XLA Modules:
  0.0 29.7 jit_solution(10638261969281600798)
XLA Ops:
  0.0 2.2 %range_edges.1 = (bf16[2,1024,384]{2,1,0:T(8,128)(2,1)S(1)}, bf16[1,1280,128]{2,1,0:T(8,128)(2,1)S(1)}, bf16[1,1280,128]{2,1,0:T(8,128)(2,1)S(1)}, bf16[2,1280,1...) custom-call(bf16[2,1024,384]{2,1,0:T(8,128)(2,1)} %x_hbm.1, ...), custom_call_target="tpu_custom_call" | custom-call | tf_op jit(solution)/shard_map/range_edges/pallas_call | solution.py:201
  2.2 0.7 %collective-permute-start = (bf16[2,1312,128]{2,1,0:T(8,128)(2,1)S(1)}, bf16[2,1312,128]{2,1,0:T(8,128)(2,1)S(1)}, u32[]{:S(2)}, u32[]{:S(2)}) collective-permute-start(bf16[2,1312,128]{2,1,0:T(8,128)(2,1)S(1)} %get-tuple-element.29), channel_id=1, source_target_pairs={{0,1},{1,0},{2,3},{3,2},{4,5},{5,4},{6,7},{7,6},{8,9},{9,8},{10,11... | collective-permute-start | bytes 2015240 | tf_op jit(solution)/shard_map/ppermute | solution.py:48
  2.9 0.1 collective-permute-start.1
  3.0 3.5 %collective-permute-start.2 = (bf16[1,1280,128]{2,1,0:T(8,128)(2,1)S(1)}, bf16[1,1280,128]{2,1,0:T(8,128)(2,1)S(1)}, u32[]{:S(2)}, u32[]{:S(2)}) collective-permute-start(bf16[1,1280,128]{2,1,0:T(8,128)(2,1)S(1)} %get-tuple-element.31), channel_id=1, source_target_pairs={{1,2},{2,1},{5,6},{6,5},{9,10},{10,9},{13,14},{14,13},{17,18},{18,... | collective-permute-start | bytes 983048 | tf_op jit(solution)/shard_map/ppermute | solution.py:48
  6.4 2.1 %collective-permute-start.3 = (bf16[1,1280,128]{2,1,0:T(8,128)(2,1)S(1)}, bf16[1,1280,128]{2,1,0:T(8,128)(2,1)S(1)}, u32[]{:S(2)}, u32[]{:S(2)}) collective-permute-start(bf16[1,1280,128]{2,1,0:T(8,128)(2,1)S(1)} %get-tuple-element.37), channel_id=1, source_target_pairs={{1,2},{2,1},{5,6},{6,5},{9,10},{10,9},{13,14},{14,13},{17,18},{18,... | collective-permute-start | bytes 983048 | tf_op jit(solution)/shard_map/ppermute | solution.py:48
  8.5 3.5 %collective-permute-start.4 = (bf16[2,1280,128]{2,1,0:T(8,128)(2,1)S(1)}, bf16[2,1280,128]{2,1,0:T(8,128)(2,1)S(1)}, u32[]{:S(2)}, u32[]{:S(2)}) collective-permute-start(bf16[2,1280,128]{2,1,0:T(8,128)(2,1)S(1)} %get-tuple-element.42), channel_id=1, source_target_pairs={{1,2},{2,1},{5,6},{6,5},{9,10},{10,9},{13,14},{14,13},{17,18},{18,... | collective-permute-start | bytes 1966088 | tf_op jit(solution)/shard_map/ppermute | solution.py:48
  12.0 0.0 collective-permute-done.2.far_ref
  12.0 0.0 collective-permute-done.core_ref
  12.0 1.3 %compress_near.1 = (bf16[2,256,384]{2,1,0:T(8,128)(2,1)S(1)}, bf16[3,256,128]{2,1,0:T(8,128)(2,1)S(1)}) custom-call(bf16[2,1024,384]{2,1,0:T(8,128)(2,1)S(1)} %get-tuple-element.28.s_ref, bf16[2,1312,128]{2,1,0:T(8,128)(2,1)S(1)} %collective-permute-done.core_ref, bf16[1,1280,128]{2,1,0:T(8,128)(2,1)S(1)} %collective-permute-done.2.far_ref, ...), custom_call_target="tpu_custom_call" | custom-call | tf_op jit(solution)/shard_map/compress_near/pallas_call | solution.py:296
  13.4 1.3 %collective-permute-start.5 = (bf16[2,256,384]{2,1,0:T(8,128)(2,1)S(1)}, bf16[2,256,384]{2,1,0:T(8,128)(2,1)S(1)}, u32[]{:S(2)}, u32[]{:S(2)}) collective-permute-start(bf16[2,256,384]{2,1,0:T(8,128)(2,1)S(1)} %get-tuple-element.43.near_ref), channel_id=1, source_target_pairs={{0,4},{4,0},{8,12},{12,8},{16,20},{20,16},{24,28},{28,24},{1,5},{5... | collective-permute-start | bytes 1179656 | tf_op jit(solution)/shard_map/ppermute | solution.py:48
  14.6 0.0 collective-permute-done.1.core_ref
  14.6 0.2 collective-permute-done.3.far_ref
  14.9 1.2 %compress_away.1.away_ref = bf16[2,256,384]{2,1,0:T(8,128)(2,1)S(1)} custom-call(bf16[2,1024,384]{2,1,0:T(8,128)(2,1)S(1)} %get-tuple-element.28.s_ref, bf16[2,1312,128]{2,1,0:T(8,128)(2,1)S(1)} %collective-permute-done.core_ref, bf16[1,1280,128]{2,1,0:T(8,128)(2,1)S(1)} %collective-permute-done.3.far_ref, bf16[1280,256]{1,0:T(8,128)(2,1)S(1)} %get-tuple-element.32.w_ref, ...), custom_call_target="tpu_custom_call" | custom-call | tf_op jit(solution)/shard_map/compress_away/pallas_call | solution.py:296
  16.0 3.3 %collective-permute-start.6 = (bf16[2,256,384]{2,1,0:T(8,128)(2,1)S(1)}, bf16[2,256,384]{2,1,0:T(8,128)(2,1)S(1)}, u32[]{:S(2)}, u32[]{:S(2)}) collective-permute-start(bf16[2,256,384]{2,1,0:T(8,128)(2,1)S(1)} %compress_away.1.away_ref), channel_id=1, source_target_pairs={{4,8},{8,4},{12,16},{16,12},{20,24},{24,20},{5,9},{9,5},{13,17},{1... | collective-permute-start | bytes 1179656 | tf_op jit(solution)/shard_map/ppermute | solution.py:48
  19.4 0.3 %azimuth_weights.1.a_ref = bf16[3,3,512,256]{3,2,1,0:T(8,128)(2,1)S(1)} custom-call(bf16[3,2,512]{2,1,0:T(2,128)(2,1)S(1)} %get-tuple-element.40.azimuth_ref), custom_call_target="tpu_custom_call" | custom-call | tf_op jit(solution)/shard_map/azimuth_weights/pallas_call | solution.py:114
  19.7 1.0 %focus_outer.1 = (f32[2,2,256,384]{3,2,1,0:T(8,128)S(1)}, f32[2,2,256,384]{3,2,1,0:T(8,128)S(1)}) custom-call(bf16[3,3,512,256]{3,2,1,0:T(8,128)(2,1)S(1)} %azimuth_weights.1.a_ref, bf16[2,256,384]{2,1,0:T(8,128)(2,1)S(1)} %get-tuple-element.43.near_ref, bf16[2,256,384]{2,1,0:T(8,128)(2,1)S(1)} %compress_away.1.away_ref), custom_call_target="tpu_custom_call" | custom-call | tf_op jit(solution)/shard_map/focus_outer/pallas_call | solution.py:349
  20.7 1.2 %collective-permute-done.4.far_ref = bf16[2,1280,128]{2,1,0:T(8,128)(2,1)S(1)} collective-permute-done((bf16[2,1280,128]{2,1,0:T(8,128)(2,1)S(1)}, bf16[2,1280,128]{2,1,0:T(8,128)(2,1)S(1)}, u32[]{:S(2)}, u32[]{:S(2)}) %collective-permute-start.4) | collective-permute-done | bytes 655392 | tf_op jit(solution)/shard_map/ppermute | solution.py:48
  21.9 2.1 %compress_mid.1.mid_ref = bf16[2,512,384]{2,1,0:T(8,128)(2,1)S(1)} custom-call(bf16[2,1024,384]{2,1,0:T(8,128)(2,1)S(1)} %get-tuple-element.28.s_ref, bf16[2,1296,128]{2,1,0:T(8,128)(2,1)S(1)} %collective-permute-done.1.core_ref, bf16[2,1280,128]{2,1,0:T(8,128)(2,1)S(1)} %collective-permute-done.4.far_ref, bf16[1280,256]{1,0:T(8,128)(2,1)S(1)} %get-tuple-element.32.w_ref, ...), custom_call_target="tpu_custom_call" | custom-call | tf_op jit(solution)/shard_map/compress_mid/pallas_call | solution.py:296
  24.0 2.0 %focus_mid.1 = (f32[2,1024,384]{2,1,0:T(8,128)}, f32[2,2,256,384]{3,2,1,0:T(8,128)S(1)}) custom-call(bf16[3,3,512,256]{3,2,1,0:T(8,128)(2,1)S(1)} %azimuth_weights.1.a_ref, bf16[2,512,384]{2,1,0:T(8,128)(2,1)S(1)} %compress_mid.1.mid_ref, f32[2,2,256,384]{3,2,1,0:T(8,128)S(1)} %get-tuple-element.47.part_ref, ...), custom_call_target="tpu_custom_call" | custom-call | tf_op jit(solution)/shard_map/focus_mid/pallas_call | solution.py:385
  26.0 1.8 %collective-permute-done.5.halo_ref = bf16[2,256,384]{2,1,0:T(8,128)(2,1)S(1)} collective-permute-done((bf16[2,256,384]{2,1,0:T(8,128)(2,1)S(1)}, bf16[2,256,384]{2,1,0:T(8,128)(2,1)S(1)}, u32[]{:S(2)}, u32[]{:S(2)}) %collective-permute-start.5) | collective-permute-done | bytes 393248 | tf_op jit(solution)/shard_map/ppermute | solution.py:48
  27.9 0.4 %near_end.1.near_ref = f32[2,256,384]{2,1,0:T(8,128)S(1)} custom-call(bf16[3,3,512,256]{3,2,1,0:T(8,128)(2,1)S(1)} %azimuth_weights.1.a_ref, f32[2,2,256,384]{3,2,1,0:T(8,128)S(1)} %get-tuple-element.49.part_ref, bf16[2,256,384]{2,1,0:T(8,128)(2,1)S(1)} %collective-permute-done.5.halo_ref), custom_call_target="tpu_custom_call" | custom-call | tf_op jit(solution)/shard_map/near_end/pallas_call | solution.py:411
  28.3 0.0 collective-permute-done.6.halo_ref
  28.3 1.3 %ends.1 = f32[2,1024,384]{2,1,0:T(8,128)} custom-call(bf16[3,3,512,256]{3,2,1,0:T(8,128)(2,1)S(1)} %azimuth_weights.1.a_ref, f32[2,2,256,384]{3,2,1,0:T(8,128)S(1)} %get-tuple-element.49.part_ref, f32[2,256,384]{2,1,0:T(8,128)S(1)} %near_end.1.near_ref, bf16[2,256,384]{2,1,0:T(8,128)(2,1)S(1)} %collective-permute-done.6.halo_ref, ...), custom_call_target="tpu_custom_call", output_to_operand_aliasing={{}: (4, {})} | custom-call | tf_op jit(solution)/shard_map/ends/pallas_call | solution.py:439
Async XLA Ops:
  2.2 9.9 %collective-permute-start = (bf16[2,1312,128]{2,1,0:T(8,128)(2,1)S(1)}, bf16[2,1312,128]{2,1,0:T(8,128)(2,1)S(1)}, u32[]{:S(2)}, u32[]{:S(2)}) collective-permute-start(bf16[2,1312,128]{2,1,0:T(8,128)(2,1)S(1)} %get-tuple-element.29), channel_id=1, source_target_pairs={{0,1},{1,0},{2,3},{3,2},{4,5},{5,4},{6,7},{7,6},{8,9},{9,8},{10,11... | collective-permute-start | bytes 2015240 | tf_op jit(solution)/shard_map/ppermute | solution.py:48
  2.9 11.7 %collective-permute-start.1 = (bf16[2,1296,128]{2,1,0:T(8,128)(2,1)S(1)}, bf16[2,1296,128]{2,1,0:T(8,128)(2,1)S(1)}, u32[]{:S(2)}, u32[]{:S(2)}) collective-permute-start(bf16[2,1296,128]{2,1,0:T(8,128)(2,1)S(1)} %get-tuple-element.30), channel_id=1, source_target_pairs={{0,1},{1,0},{2,3},{3,2},{4,5},{5,4},{6,7},{7,6},{8,9},{9,8},{10,11... | collective-permute-start | bytes 1990664 | tf_op jit(solution)/shard_map/ppermute | solution.py:48
  3.0 9.0 %collective-permute-start.2 = (bf16[1,1280,128]{2,1,0:T(8,128)(2,1)S(1)}, bf16[1,1280,128]{2,1,0:T(8,128)(2,1)S(1)}, u32[]{:S(2)}, u32[]{:S(2)}) collective-permute-start(bf16[1,1280,128]{2,1,0:T(8,128)(2,1)S(1)} %get-tuple-element.31), channel_id=1, source_target_pairs={{1,2},{2,1},{5,6},{6,5},{9,10},{10,9},{13,14},{14,13},{17,18},{18,... | collective-permute-start | bytes 983048 | tf_op jit(solution)/shard_map/ppermute | solution.py:48
  6.4 8.4 %collective-permute-start.3 = (bf16[1,1280,128]{2,1,0:T(8,128)(2,1)S(1)}, bf16[1,1280,128]{2,1,0:T(8,128)(2,1)S(1)}, u32[]{:S(2)}, u32[]{:S(2)}) collective-permute-start(bf16[1,1280,128]{2,1,0:T(8,128)(2,1)S(1)} %get-tuple-element.37), channel_id=1, source_target_pairs={{1,2},{2,1},{5,6},{6,5},{9,10},{10,9},{13,14},{14,13},{17,18},{18,... | collective-permute-start | bytes 983048 | tf_op jit(solution)/shard_map/ppermute | solution.py:48
  8.5 13.3 %collective-permute-start.4 = (bf16[2,1280,128]{2,1,0:T(8,128)(2,1)S(1)}, bf16[2,1280,128]{2,1,0:T(8,128)(2,1)S(1)}, u32[]{:S(2)}, u32[]{:S(2)}) collective-permute-start(bf16[2,1280,128]{2,1,0:T(8,128)(2,1)S(1)} %get-tuple-element.42), channel_id=1, source_target_pairs={{1,2},{2,1},{5,6},{6,5},{9,10},{10,9},{13,14},{14,13},{17,18},{18,... | collective-permute-start | bytes 1966088 | tf_op jit(solution)/shard_map/ppermute | solution.py:48
  13.4 14.5 %collective-permute-start.5 = (bf16[2,256,384]{2,1,0:T(8,128)(2,1)S(1)}, bf16[2,256,384]{2,1,0:T(8,128)(2,1)S(1)}, u32[]{:S(2)}, u32[]{:S(2)}) collective-permute-start(bf16[2,256,384]{2,1,0:T(8,128)(2,1)S(1)} %get-tuple-element.43.near_ref), channel_id=1, source_target_pairs={{0,4},{4,0},{8,12},{12,8},{16,20},{20,16},{24,28},{28,24},{1,5},{5... | collective-permute-start | bytes 1179656 | tf_op jit(solution)/shard_map/ppermute | solution.py:48
  16.0 12.2 %collective-permute-start.6 = (bf16[2,256,384]{2,1,0:T(8,128)(2,1)S(1)}, bf16[2,256,384]{2,1,0:T(8,128)(2,1)S(1)}, u32[]{:S(2)}, u32[]{:S(2)}) collective-permute-start(bf16[2,256,384]{2,1,0:T(8,128)(2,1)S(1)} %compress_away.1.away_ref), channel_id=1, source_target_pairs={{4,8},{8,4},{12,16},{16,12},{20,24},{24,20},{5,9},{9,5},{13,17},{1... | collective-permute-start | bytes 1179656 | tf_op jit(solution)/shard_map/ppermute | solution.py:48

commit v5 on v3

--- a/solution.py
+++ b/solution.py
@@ -83,7 +83,7 @@
     for b in range(blocks):
         source = lax.broadcasted_iota(jnp.int32, (span, LANES), 0)
         column = lax.broadcasted_iota(jnp.int32, (span, LANES), 1)
-        tap = source - column - (HALF - tap_count // 2) - shift_ref[b][:1, :]
+        tap = source - column - (HALF - tap_count // 2) - shift_ref[b]
         place = source + first + b * LANES
         tap = jnp.where((place >= 0) & (place < total), tap, -1)
         matrix = jnp.zeros((span, LANES), F32)
@@ -154,7 +154,7 @@
 def edges_kernel(
     x_hbm, range_hbm, taps_hbm, shift_hbm, azimuth_hbm,
     x_ref, far_near_ref, far_away_ref, far_mid_ref, core_outer_ref, core_mid_ref,
-    w_ref, taps_ref, splat_ref, azimuth_ref, range_ref, shift_ref, sems,
+    w_ref, m_ref, azimuth_ref, range_ref, taps_ref, shift_ref, sems,
 ):
     rows = x_ref.shape[1]
     near, away = near_away_rows(rows)
@@ -181,8 +181,7 @@
         extra = ref.shape[1] - 5 * CHUNK
         ref[:, 5 * CHUNK :, :] = jnp.zeros((ref.shape[0], extra, LANES), BF16)
     range_toeplitz(range_ref, w_ref)
-    for b in range(splat_ref.shape[0]):
-        splat_ref[b] = jnp.full(splat_ref.shape[1:], shift_ref[b], jnp.int32)
+    migration_bands(taps_ref, shift_ref, m_ref)
 
     def body(odd):
         for i, start in enumerate(starts):
@@ -209,14 +208,14 @@
         )
         + (
             jax.ShapeDtypeStruct((2 * depth, 2 * LANES), BF16),
-            jax.ShapeDtypeStruct(migration_taps.shape, BF16),
-            jax.ShapeDtypeStruct((blocks, 8, LANES), jnp.int32),
+            jax.ShapeDtypeStruct((blocks, 2 * LANES, LANES), BF16),
             jax.ShapeDtypeStruct(azimuth_chirp.shape, BF16),
         ),
         in_specs=[pl.BlockSpec(memory_space=pltpu.HBM)] * len(args),
-        out_specs=(pl.BlockSpec(memory_space=pltpu.VMEM),) * 10,
+        out_specs=(pl.BlockSpec(memory_space=pltpu.VMEM),) * 9,
         scratch_shapes=[
             pltpu.VMEM(range_chirp.shape, BF16),
+            pltpu.VMEM(migration_taps.shape, BF16),
             pltpu.SMEM(block_shift.shape, jnp.int32),
             pltpu.SemaphoreType.DMA((chunks + len(args) - 1,)),
         ],
@@ -266,18 +265,15 @@
 
 def compress_kernel(which, s_ref, core_ref, far_ref, w_ref, *refs):
     near, away = near_away_rows(s_ref.shape[1])
+    m_ref, out_ref, *c_refs = refs
     if which == "near":
-        taps_ref, splat_ref, out_ref, m_ref, *c_refs = refs
         jobs = [(near, 0)]
     else:
-        m_ref, out_ref, *c_refs = refs
         jobs = [(CHUNK * (i + 1), i) for i in range(out_ref.shape[1] // CHUNK)]
         if which == "away":
             jobs = [(away, 1)]
 
     def body(odd):
-        if which == "near":
-            migration_bands(taps_ref, splat_ref, m_ref)
         for i, (start, chunk) in enumerate(jobs):
             core, far = (core_ref, chunk), (far_ref, chunk if which == "mid" else 0)
             left, right = (core, far) if odd else (far, core)
@@ -293,8 +289,6 @@
     count = rows // CHUNK - 2 if which == "mid" else 1
     args = (echo, core, far, w) + bands
     out = (jax.ShapeDtypeStruct((2, count * CHUNK, cells), BF16),)
-    if which == "near":
-        out += (jax.ShapeDtypeStruct((cells // LANES, 2 * LANES, LANES), BF16),)
     result = pl.pallas_call(
         functools.partial(compress_kernel, which),
         out_shape=out,
@@ -304,7 +298,7 @@
         compiler_params=params(),
         name="compress_" + which,
     )(*args)
-    return result if which == "near" else result[0]
+    return result[0]
 
 
 def lines(ref, chunk):
@@ -422,14 +416,33 @@
 
 def ends_kernel(a_ref, part_ref, near_ref, halo_ref, _, image_ref, sum_ref, sems):
     rows = image_ref.shape[1]
+    half = CHUNK // 2
 
     def body(odd):
-        copies = []
-        for i, (source, end) in enumerate(((near_ref, 1 - odd), (sum_ref, odd))):
-            if i == 1:
-                add_halo(a_ref, end, part_ref, halo_ref, sum_ref)
-            target = image_ref.at[:, pl.ds(end * (rows - CHUNK), CHUNK), :]
-            copies.append(pltpu.make_async_copy(source, target, sems.at[i]))
+        near_first, away_first = (1 - odd) * (rows - CHUNK), odd * (rows - CHUNK)
+        copies = [
+            pltpu.make_async_copy(
+                near_ref, image_ref.at[:, pl.ds(near_first, CHUNK), :], sems.at[2]
+            )
+        ]
+        copies[0].start()
+        window = lines(halo_ref, 0)
+        for h in range(2):
+            picked = slice(h * half, (h + 1) * half)
+            for b in range(a_ref.shape[1]):
+                taps = jnp.concatenate(
+                    [a_ref[2 * odd, b, base + h * half : base + (h + 1) * half] for base in (0, CHUNK)],
+                    axis=0,
+                )
+                both = jnp.concatenate([window(0, tile_of(b)), window(1, tile_of(b))], axis=1)
+                result = jnp.dot(taps, both, preferred_element_type=F32)
+                top, bottom = result[:half], result[half:]
+                real = top[:, :LANES] + bottom[:, LANES:]
+                imag = top[:, LANES:] - bottom[:, :LANES]
+                sum_ref[0, picked, tile_of(b)] = part_ref[odd, 0, picked, tile_of(b)] + real
+                sum_ref[1, picked, tile_of(b)] = part_ref[odd, 1, picked, tile_of(b)] + imag
+            target = image_ref.at[:, pl.ds(away_first + h * half, half), :]
+            copies.append(pltpu.make_async_copy(sum_ref.at[:, picked, :], target, sems.at[h]))
             copies[-1].start()
         for copy in copies:
             copy.wait()
@@ -444,7 +457,7 @@
         in_specs=[pl.BlockSpec(memory_space=pltpu.VMEM)] * 4
         + [pl.BlockSpec(memory_space=pl.ANY)],
         out_specs=pl.BlockSpec(memory_space=pl.ANY),
-        scratch_shapes=[pltpu.VMEM(near.shape, F32), pltpu.SemaphoreType.DMA((2,))],
+        scratch_shapes=[pltpu.VMEM(near.shape, F32), pltpu.SemaphoreType.DMA((3,))],
         input_output_aliases={4: 0},
         compiler_params=params(),
         name="ends",
@@ -452,7 +465,7 @@
 
 
 def per_device(raw_echo, range_chirp, migration_taps, block_shift, azimuth_chirp):
-    echo, far_near, far_away, far_mid, core_outer, core_mid, w, taps, splat, azimuth_chirp = range_edges(
+    echo, far_near, far_away, far_mid, core_outer, core_mid, w, m, azimuth_chirp = range_edges(
         raw_echo, range_chirp, migration_taps, block_shift, azimuth_chirp
     )
     core_outer = swap(core_outer, "rg", 0)
@@ -460,7 +473,7 @@
     far_near = swap(far_near, "rg", 1)
     far_away = swap(far_away, "rg", 1)
     far_mid = swap(far_mid, "rg", 1)
-    near, m = compress("near", echo, core_outer, far_near, w, taps, splat)
+    near = compress("near", echo, core_outer, far_near, w, m)
     near_halo = swap(near, "az", 0)
     core_outer, core_mid, near = lax.optimization_barrier((core_outer, core_mid, near))
     away = compress("away", echo, core_outer, far_away, w, m)

time: 29.6 us -> 29.7 us (level)
  no operation moved by 1% of the time
where the time goes in v5:
time: 29.7 us; the launch traced here: 29.5 us
  starting transfers between devices  14.4 us (48%)
  Pallas kernels  11.5 us (39%)
  waiting for transfers between devices  3.29 us (11%)
    ppermute x7, starting transfers between devices, swap(): return lax.ppermute(x, axis, swap_pairs(lax.axis_size(axis), first))  14.4 us
    pallas_call x3, Pallas kernels, compress(): pl.pallas_call(functools.partial(compress_kernel, which), out_shape=out,...  4.48 us
    ppermute x7, waiting for transfers between devices, swap(): return lax.ppermute(x, axis, swap_pairs(lax.axis_size(axis), first))  3.29 us
    pallas_call x1, Pallas kernels, range_edges(): pl.pallas_call(edges_kernel, out_shape=(jax.ShapeDtypeStruct(raw.shape, B...  2.1 us
    pallas_call x1, Pallas kernels, focus_mid(): pl.pallas_call(focus_mid_kernel, out_shape=(jax.ShapeDtypeStruct((2, (mid...  2.02 us
    pallas_call x1, Pallas kernels, ends(): pl.pallas_call(ends_kernel, out_shape=jax.ShapeDtypeStruct(image.shape, F...  1.23 us
    pallas_call x1, Pallas kernels, focus_outer(): pl.pallas_call(focus_outer_kernel, out_shape=(jax.ShapeDtypeStruct((2, 2,...  1.01 us
  transfers between devices with their start and end apart: 7, of which 3 were waited for; matrix products, arithmetic and copies ran while one was open for 0% of the time, Pallas kernels for 28%

profile of v5, /device:TPU:17, one launch (start us, length us, event | category | flops | bytes accessed | tf_op | source)
XLA Modules:
  0.0 29.5 jit_solution(9215604531363674701)
XLA Ops:
  0.0 2.1 %range_edges.1 = (bf16[2,1024,384]{2,1,0:T(8,128)(2,1)S(1)}, bf16[1,1280,128]{2,1,0:T(8,128)(2,1)S(1)}, bf16[1,1280,128]{2,1,0:T(8,128)(2,1)S(1)}, bf16[2,1280,1...) custom-call(bf16[2,1024,384]{2,1,0:T(8,128)(2,1)} %x_hbm.1, ...), custom_call_target="tpu_custom_call" | custom-call | tf_op jit(solution)/shard_map/range_edges/pallas_call | solution.py:202
  2.1 0.7 %collective-permute-start = (bf16[2,1312,128]{2,1,0:T(8,128)(2,1)S(1)}, bf16[2,1312,128]{2,1,0:T(8,128)(2,1)S(1)}, u32[]{:S(2)}, u32[]{:S(2)}) collective-permute-start(bf16[2,1312,128]{2,1,0:T(8,128)(2,1)S(1)} %get-tuple-element.26), channel_id=1, source_target_pairs={{0,1},{1,0},{2,3},{3,2},{4,5},{5,4},{6,7},{7,6},{8,9},{9,8},{10,11... | collective-permute-start | bytes 2015240 | tf_op jit(solution)/shard_map/ppermute | solution.py:48
  2.8 0.1 collective-permute-start.1
  2.9 3.5 %collective-permute-start.2 = (bf16[1,1280,128]{2,1,0:T(8,128)(2,1)S(1)}, bf16[1,1280,128]{2,1,0:T(8,128)(2,1)S(1)}, u32[]{:S(2)}, u32[]{:S(2)}) collective-permute-start(bf16[1,1280,128]{2,1,0:T(8,128)(2,1)S(1)} %get-tuple-element.28), channel_id=1, source_target_pairs={{1,2},{2,1},{5,6},{6,5},{9,10},{10,9},{13,14},{14,13},{17,18},{18,... | collective-permute-start | bytes 983048 | tf_op jit(solution)/shard_map/ppermute | solution.py:48
  6.4 2.1 %collective-permute-start.3 = (bf16[1,1280,128]{2,1,0:T(8,128)(2,1)S(1)}, bf16[1,1280,128]{2,1,0:T(8,128)(2,1)S(1)}, u32[]{:S(2)}, u32[]{:S(2)}) collective-permute-start(bf16[1,1280,128]{2,1,0:T(8,128)(2,1)S(1)} %get-tuple-element.32), channel_id=1, source_target_pairs={{1,2},{2,1},{5,6},{6,5},{9,10},{10,9},{13,14},{14,13},{17,18},{18,... | collective-permute-start | bytes 983048 | tf_op jit(solution)/shard_map/ppermute | solution.py:48
  8.5 3.5 %collective-permute-start.4 = (bf16[2,1280,128]{2,1,0:T(8,128)(2,1)S(1)}, bf16[2,1280,128]{2,1,0:T(8,128)(2,1)S(1)}, u32[]{:S(2)}, u32[]{:S(2)}) collective-permute-start(bf16[2,1280,128]{2,1,0:T(8,128)(2,1)S(1)} %get-tuple-element.36), channel_id=1, source_target_pairs={{1,2},{2,1},{5,6},{6,5},{9,10},{10,9},{13,14},{14,13},{17,18},{18,... | collective-permute-start | bytes 1966088 | tf_op jit(solution)/shard_map/ppermute | solution.py:48
  11.9 0.0 collective-permute-done.2.far_ref
  12.0 0.0 collective-permute-done.core_ref
  12.0 1.2 %compress_near.1.near_ref = bf16[2,256,384]{2,1,0:T(8,128)(2,1)S(1)} custom-call(bf16[2,1024,384]{2,1,0:T(8,128)(2,1)S(1)} %get-tuple-element.25.s_ref, bf16[2,1312,128]{2,1,0:T(8,128)(2,1)S(1)} %collective-permute-done.core_ref, bf16[1,1280,128]{2,1,0:T(8,128)(2,1)S(1)} %collective-permute-done.2.far_ref, bf16[1280,256]{1,0:T(8,128)(2,1)S(1)} %get-tuple-element.29.w_ref, ...), custom_call_target="tpu_custom_call" | custom-call | tf_op jit(solution)/shard_map/compress_near/pallas_call | solution.py:292
  13.2 1.3 %collective-permute-start.5 = (bf16[2,256,384]{2,1,0:T(8,128)(2,1)S(1)}, bf16[2,256,384]{2,1,0:T(8,128)(2,1)S(1)}, u32[]{:S(2)}, u32[]{:S(2)}) collective-permute-start(bf16[2,256,384]{2,1,0:T(8,128)(2,1)S(1)} %compress_near.1.near_ref), channel_id=1, source_target_pairs={{0,4},{4,0},{8,12},{12,8},{16,20},{20,16},{24,28},{28,24},{1,5},{5... | collective-permute-start | bytes 1179656 | tf_op jit(solution)/shard_map/ppermute | solution.py:48
  14.4 0.0 collective-permute-done.1.core_ref
  14.4 0.4 %collective-permute-done.3.far_ref = bf16[1,1280,128]{2,1,0:T(8,128)(2,1)S(1)} collective-permute-done((bf16[1,1280,128]{2,1,0:T(8,128)(2,1)S(1)}, bf16[1,1280,128]{2,1,0:T(8,128)(2,1)S(1)}, u32[]{:S(2)}, u32[]{:S(2)}) %collective-permute-start.3) | collective-permute-done | bytes 327712 | tf_op jit(solution)/shard_map/ppermute | solution.py:48
  14.8 1.2 %compress_away.1.away_ref = bf16[2,256,384]{2,1,0:T(8,128)(2,1)S(1)} custom-call(bf16[2,1024,384]{2,1,0:T(8,128)(2,1)S(1)} %get-tuple-element.25.s_ref, bf16[2,1312,128]{2,1,0:T(8,128)(2,1)S(1)} %collective-permute-done.core_ref, bf16[1,1280,128]{2,1,0:T(8,128)(2,1)S(1)} %collective-permute-done.3.far_ref, bf16[1280,256]{1,0:T(8,128)(2,1)S(1)} %get-tuple-element.29.w_ref, ...), custom_call_target="tpu_custom_call" | custom-call | tf_op jit(solution)/shard_map/compress_away/pallas_call | solution.py:292
  16.0 3.3 %collective-permute-start.6 = (bf16[2,256,384]{2,1,0:T(8,128)(2,1)S(1)}, bf16[2,256,384]{2,1,0:T(8,128)(2,1)S(1)}, u32[]{:S(2)}, u32[]{:S(2)}) collective-permute-start(bf16[2,256,384]{2,1,0:T(8,128)(2,1)S(1)} %compress_away.1.away_ref), channel_id=1, source_target_pairs={{4,8},{8,4},{12,16},{16,12},{20,24},{24,20},{5,9},{9,5},{13,17},{1... | collective-permute-start | bytes 1179656 | tf_op jit(solution)/shard_map/ppermute | solution.py:48
  19.3 0.3 %azimuth_weights.1.a_ref = bf16[3,3,512,256]{3,2,1,0:T(8,128)(2,1)S(1)} custom-call(bf16[3,2,512]{2,1,0:T(2,128)(2,1)S(1)} %get-tuple-element.34.azimuth_ref), custom_call_target="tpu_custom_call" | custom-call | tf_op jit(solution)/shard_map/azimuth_weights/pallas_call | solution.py:114
  19.6 1.0 %focus_outer.1 = (f32[2,2,256,384]{3,2,1,0:T(8,128)S(1)}, f32[2,2,256,384]{3,2,1,0:T(8,128)S(1)}) custom-call(bf16[3,3,512,256]{3,2,1,0:T(8,128)(2,1)S(1)} %azimuth_weights.1.a_ref, bf16[2,256,384]{2,1,0:T(8,128)(2,1)S(1)} %compress_near.1.near_ref, bf16[2,256,384]{2,1,0:T(8,128)(2,1)S(1)} %compress_away.1.away_ref), custom_call_target="tpu_custom_call" | custom-call | tf_op jit(solution)/shard_map/focus_outer/pallas_call | solution.py:345
  20.6 1.2 %collective-permute-done.4.far_ref = bf16[2,1280,128]{2,1,0:T(8,128)(2,1)S(1)} collective-permute-done((bf16[2,1280,128]{2,1,0:T(8,128)(2,1)S(1)}, bf16[2,1280,128]{2,1,0:T(8,128)(2,1)S(1)}, u32[]{:S(2)}, u32[]{:S(2)}) %collective-permute-start.4) | collective-permute-done | bytes 655392 | tf_op jit(solution)/shard_map/ppermute | solution.py:48
  21.8 2.1 %compress_mid.1.mid_ref = bf16[2,512,384]{2,1,0:T(8,128)(2,1)S(1)} custom-call(bf16[2,1024,384]{2,1,0:T(8,128)(2,1)S(1)} %get-tuple-element.25.s_ref, bf16[2,1296,128]{2,1,0:T(8,128)(2,1)S(1)} %collective-permute-done.1.core_ref, bf16[2,1280,128]{2,1,0:T(8,128)(2,1)S(1)} %collective-permute-done.4.far_ref, bf16[1280,256]{1,0:T(8,128)(2,1)S(1)} %get-tuple-element.29.w_ref, ...), custom_call_target="tpu_custom_call" | custom-call | tf_op jit(solution)/shard_map/compress_mid/pallas_call | solution.py:292
  23.9 2.0 %focus_mid.1 = (f32[2,1024,384]{2,1,0:T(8,128)}, f32[2,2,256,384]{3,2,1,0:T(8,128)S(1)}) custom-call(bf16[3,3,512,256]{3,2,1,0:T(8,128)(2,1)S(1)} %azimuth_weights.1.a_ref, bf16[2,512,384]{2,1,0:T(8,128)(2,1)S(1)} %compress_mid.1.mid_ref, f32[2,2,256,384]{3,2,1,0:T(8,128)S(1)} %get-tuple-element.41.part_ref, ...), custom_call_target="tpu_custom_call" | custom-call | tf_op jit(solution)/shard_map/focus_mid/pallas_call | solution.py:381
  26.0 1.7 %collective-permute-done.5.halo_ref = bf16[2,256,384]{2,1,0:T(8,128)(2,1)S(1)} collective-permute-done((bf16[2,256,384]{2,1,0:T(8,128)(2,1)S(1)}, bf16[2,256,384]{2,1,0:T(8,128)(2,1)S(1)}, u32[]{:S(2)}, u32[]{:S(2)}) %collective-permute-start.5) | collective-permute-done | bytes 393248 | tf_op jit(solution)/shard_map/ppermute | solution.py:48
  27.7 0.4 %near_end.1.near_ref = f32[2,256,384]{2,1,0:T(8,128)S(1)} custom-call(bf16[3,3,512,256]{3,2,1,0:T(8,128)(2,1)S(1)} %azimuth_weights.1.a_ref, f32[2,2,256,384]{3,2,1,0:T(8,128)S(1)} %get-tuple-element.43.part_ref, bf16[2,256,384]{2,1,0:T(8,128)(2,1)S(1)} %collective-permute-done.5.halo_ref), custom_call_target="tpu_custom_call" | custom-call | tf_op jit(solution)/shard_map/near_end/pallas_call | solution.py:407
  28.1 0.0 collective-permute-done.6.halo_ref
  28.1 1.2 %ends.1 = f32[2,1024,384]{2,1,0:T(8,128)} custom-call(bf16[3,3,512,256]{3,2,1,0:T(8,128)(2,1)S(1)} %azimuth_weights.1.a_ref, f32[2,2,256,384]{3,2,1,0:T(8,128)S(1)} %get-tuple-element.43.part_ref, f32[2,256,384]{2,1,0:T(8,128)S(1)} %near_end.1.near_ref, bf16[2,256,384]{2,1,0:T(8,128)(2,1)S(1)} %collective-permute-done.6.halo_ref, ...), custom_call_target="tpu_custom_call", output_to_operand_aliasing={{}: (4, {})} | custom-call | tf_op jit(solution)/shard_map/ends/pallas_call | solution.py:454
Async XLA Ops:
  2.1 9.9 %collective-permute-start = (bf16[2,1312,128]{2,1,0:T(8,128)(2,1)S(1)}, bf16[2,1312,128]{2,1,0:T(8,128)(2,1)S(1)}, u32[]{:S(2)}, u32[]{:S(2)}) collective-permute-start(bf16[2,1312,128]{2,1,0:T(8,128)(2,1)S(1)} %get-tuple-element.26), channel_id=1, source_target_pairs={{0,1},{1,0},{2,3},{3,2},{4,5},{5,4},{6,7},{7,6},{8,9},{9,8},{10,11... | collective-permute-start | bytes 2015240 | tf_op jit(solution)/shard_map/ppermute | solution.py:48
  2.8 11.6 %collective-permute-start.1 = (bf16[2,1296,128]{2,1,0:T(8,128)(2,1)S(1)}, bf16[2,1296,128]{2,1,0:T(8,128)(2,1)S(1)}, u32[]{:S(2)}, u32[]{:S(2)}) collective-permute-start(bf16[2,1296,128]{2,1,0:T(8,128)(2,1)S(1)} %get-tuple-element.27), channel_id=1, source_target_pairs={{0,1},{1,0},{2,3},{3,2},{4,5},{5,4},{6,7},{7,6},{8,9},{9,8},{10,11... | collective-permute-start | bytes 1990664 | tf_op jit(solution)/shard_map/ppermute | solution.py:48
  2.9 9.0 %collective-permute-start.2 = (bf16[1,1280,128]{2,1,0:T(8,128)(2,1)S(1)}, bf16[1,1280,128]{2,1,0:T(8,128)(2,1)S(1)}, u32[]{:S(2)}, u32[]{:S(2)}) collective-permute-start(bf16[1,1280,128]{2,1,0:T(8,128)(2,1)S(1)} %get-tuple-element.28), channel_id=1, source_target_pairs={{1,2},{2,1},{5,6},{6,5},{9,10},{10,9},{13,14},{14,13},{17,18},{18,... | collective-permute-start | bytes 983048 | tf_op jit(solution)/shard_map/ppermute | solution.py:48
  6.4 8.4 %collective-permute-start.3 = (bf16[1,1280,128]{2,1,0:T(8,128)(2,1)S(1)}, bf16[1,1280,128]{2,1,0:T(8,128)(2,1)S(1)}, u32[]{:S(2)}, u32[]{:S(2)}) collective-permute-start(bf16[1,1280,128]{2,1,0:T(8,128)(2,1)S(1)} %get-tuple-element.32), channel_id=1, source_target_pairs={{1,2},{2,1},{5,6},{6,5},{9,10},{10,9},{13,14},{14,13},{17,18},{18,... | collective-permute-start | bytes 983048 | tf_op jit(solution)/shard_map/ppermute | solution.py:48
  8.5 13.3 %collective-permute-start.4 = (bf16[2,1280,128]{2,1,0:T(8,128)(2,1)S(1)}, bf16[2,1280,128]{2,1,0:T(8,128)(2,1)S(1)}, u32[]{:S(2)}, u32[]{:S(2)}) collective-permute-start(bf16[2,1280,128]{2,1,0:T(8,128)(2,1)S(1)} %get-tuple-element.36), channel_id=1, source_target_pairs={{1,2},{2,1},{5,6},{6,5},{9,10},{10,9},{13,14},{14,13},{17,18},{18,... | collective-permute-start | bytes 1966088 | tf_op jit(solution)/shard_map/ppermute | solution.py:48
  13.2 14.5 %collective-permute-start.5 = (bf16[2,256,384]{2,1,0:T(8,128)(2,1)S(1)}, bf16[2,256,384]{2,1,0:T(8,128)(2,1)S(1)}, u32[]{:S(2)}, u32[]{:S(2)}) collective-permute-start(bf16[2,256,384]{2,1,0:T(8,128)(2,1)S(1)} %compress_near.1.near_ref), channel_id=1, source_target_pairs={{0,4},{4,0},{8,12},{12,8},{16,20},{20,16},{24,28},{28,24},{1,5},{5... | collective-permute-start | bytes 1179656 | tf_op jit(solution)/shard_map/ppermute | solution.py:48
  16.0 12.1 %collective-permute-start.6 = (bf16[2,256,384]{2,1,0:T(8,128)(2,1)S(1)}, bf16[2,256,384]{2,1,0:T(8,128)(2,1)S(1)}, u32[]{:S(2)}, u32[]{:S(2)}) collective-permute-start(bf16[2,256,384]{2,1,0:T(8,128)(2,1)S(1)} %compress_away.1.away_ref), channel_id=1, source_target_pairs={{4,8},{8,4},{12,16},{16,12},{20,24},{24,20},{5,9},{9,5},{13,17},{1... | collective-permute-start | bytes 1179656 | tf_op jit(solution)/shard_map/ppermute | solution.py:48

commit v6 on v5

--- a/solution.py
+++ b/solution.py
@@ -83,7 +83,7 @@
     for b in range(blocks):
         source = lax.broadcasted_iota(jnp.int32, (span, LANES), 0)
         column = lax.broadcasted_iota(jnp.int32, (span, LANES), 1)
-        tap = source - column - (HALF - tap_count // 2) - shift_ref[b]
+        tap = source - column - (HALF - tap_count // 2) - shift_ref[b][:1, :]
         place = source + first + b * LANES
         tap = jnp.where((place >= 0) & (place < total), tap, -1)
         matrix = jnp.zeros((span, LANES), F32)
@@ -154,7 +154,7 @@
 def edges_kernel(
     x_hbm, range_hbm, taps_hbm, shift_hbm, azimuth_hbm,
     x_ref, far_near_ref, far_away_ref, far_mid_ref, core_outer_ref, core_mid_ref,
-    w_ref, m_ref, azimuth_ref, range_ref, taps_ref, shift_ref, sems,
+    w_ref, taps_ref, splat_ref, azimuth_ref, range_ref, shift_ref, sems,
 ):
     rows = x_ref.shape[1]
     near, away = near_away_rows(rows)
@@ -181,7 +181,8 @@
         extra = ref.shape[1] - 5 * CHUNK
         ref[:, 5 * CHUNK :, :] = jnp.zeros((ref.shape[0], extra, LANES), BF16)
     range_toeplitz(range_ref, w_ref)
-    migration_bands(taps_ref, shift_ref, m_ref)
+    for b in range(splat_ref.shape[0]):
+        splat_ref[b] = jnp.full(splat_ref.shape[1:], shift_ref[b], jnp.int32)
 
     def body(odd):
         for i, start in enumerate(starts):
@@ -208,14 +209,14 @@
         )
         + (
             jax.ShapeDtypeStruct((2 * depth, 2 * LANES), BF16),
-            jax.ShapeDtypeStruct((blocks, 2 * LANES, LANES), BF16),
+            jax.ShapeDtypeStruct(migration_taps.shape, BF16),
+            jax.ShapeDtypeStruct((blocks, 8, LANES), jnp.int32),
             jax.ShapeDtypeStruct(azimuth_chirp.shape, BF16),
         ),
         in_specs=[pl.BlockSpec(memory_space=pltpu.HBM)] * len(args),
-        out_specs=(pl.BlockSpec(memory_space=pltpu.VMEM),) * 9,
+        out_specs=(pl.BlockSpec(memory_space=pltpu.VMEM),) * 10,
         scratch_shapes=[
             pltpu.VMEM(range_chirp.shape, BF16),
-            pltpu.VMEM(migration_taps.shape, BF16),
             pltpu.SMEM(block_shift.shape, jnp.int32),
             pltpu.SemaphoreType.DMA((chunks + len(args) - 1,)),
         ],
@@ -265,15 +266,18 @@
 
 def compress_kernel(which, s_ref, core_ref, far_ref, w_ref, *refs):
     near, away = near_away_rows(s_ref.shape[1])
-    m_ref, out_ref, *c_refs = refs
     if which == "near":
+        taps_ref, splat_ref, out_ref, m_ref, *c_refs = refs
         jobs = [(near, 0)]
     else:
+        m_ref, out_ref, *c_refs = refs
         jobs = [(CHUNK * (i + 1), i) for i in range(out_ref.shape[1] // CHUNK)]
         if which == "away":
             jobs = [(away, 1)]
 
     def body(odd):
+        if which == "near":
+            migration_bands(taps_ref, splat_ref, m_ref)
         for i, (start, chunk) in enumerate(jobs):
             core, far = (core_ref, chunk), (far_ref, chunk if which == "mid" else 0)
             left, right = (core, far) if odd else (far, core)
@@ -289,6 +293,8 @@
     count = rows // CHUNK - 2 if which == "mid" else 1
     args = (echo, core, far, w) + bands
     out = (jax.ShapeDtypeStruct((2, count * CHUNK, cells), BF16),)
+    if which == "near":
+        out += (jax.ShapeDtypeStruct((cells // LANES, 2 * LANES, LANES), BF16),)
     result = pl.pallas_call(
         functools.partial(compress_kernel, which),
         out_shape=out,
@@ -298,7 +304,7 @@
         compiler_params=params(),
         name="compress_" + which,
     )(*args)
-    return result[0]
+    return result if which == "near" else result[0]
 
 
 def lines(ref, chunk):
@@ -465,7 +471,7 @@
 
 
 def per_device(raw_echo, range_chirp, migration_taps, block_shift, azimuth_chirp):
-    echo, far_near, far_away, far_mid, core_outer, core_mid, w, m, azimuth_chirp = range_edges(
+    echo, far_near, far_away, far_mid, core_outer, core_mid, w, taps, splat, azimuth_chirp = range_edges(
         raw_echo, range_chirp, migration_taps, block_shift, azimuth_chirp
     )
     core_outer = swap(core_outer, "rg", 0)
@@ -473,7 +479,7 @@
     far_near = swap(far_near, "rg", 1)
     far_away = swap(far_away, "rg", 1)
     far_mid = swap(far_mid, "rg", 1)
-    near = compress("near", echo, core_outer, far_near, w, m)
+    near, m = compress("near", echo, core_outer, far_near, w, taps, splat)
     near_halo = swap(near, "az", 0)
     core_outer, core_mid, near = lax.optimization_barrier((core_outer, core_mid, near))
     away = compress("away", echo, core_outer, far_away, w, m)

time: 29.7 us -> 29.5 us (level)
  no operation moved by 1% of the time
where the time goes in v6:
time: 29.5 us; the launch traced here: 29.3 us
  starting transfers between devices  14.4 us (49%)
  Pallas kernels  11.4 us (39%)
  waiting for transfers between devices  3.3 us (11%)
    ppermute x7, starting transfers between devices, swap(): return lax.ppermute(x, axis, swap_pairs(lax.axis_size(axis), first))  14.4 us
    pallas_call x3, Pallas kernels, compress(): pl.pallas_call(functools.partial(compress_kernel, which), out_shape=out,...  4.61 us
    ppermute x7, waiting for transfers between devices, swap(): return lax.ppermute(x, axis, swap_pairs(lax.axis_size(axis), first))  3.3 us
    pallas_call x1, Pallas kernels, focus_mid(): pl.pallas_call(focus_mid_kernel, out_shape=(jax.ShapeDtypeStruct((2, (mid...  2.02 us
    pallas_call x1, Pallas kernels, range_edges(): pl.pallas_call(edges_kernel, out_shape=(jax.ShapeDtypeStruct(raw.shape, B...  1.82 us
    pallas_call x1, Pallas kernels, ends(): pl.pallas_call(ends_kernel, out_shape=jax.ShapeDtypeStruct(image.shape, F...  1.22 us
    pallas_call x1, Pallas kernels, focus_outer(): pl.pallas_call(focus_outer_kernel, out_shape=(jax.ShapeDtypeStruct((2, 2,...  1 us
  transfers between devices with their start and end apart: 7, of which 3 were waited for; matrix products, arithmetic and copies ran while one was open for 0% of the time, Pallas kernels for 28%

profile of v6, /device:TPU:17, one launch (start us, length us, event | category | flops | bytes accessed | tf_op | source)
XLA Modules:
  0.0 29.3 jit_solution(15127837415004304798)
XLA Ops:
  0.0 1.8 %range_edges.1 = (bf16[2,1024,384]{2,1,0:T(8,128)(2,1)S(1)}, bf16[1,1280,128]{2,1,0:T(8,128)(2,1)S(1)}, bf16[1,1280,128]{2,1,0:T(8,128)(2,1)S(1)}, bf16[2,1280,1...) custom-call(bf16[2,1024,384]{2,1,0:T(8,128)(2,1)} %x_hbm.1, ...), custom_call_target="tpu_custom_call" | custom-call | tf_op jit(solution)/shard_map/range_edges/pallas_call | solution.py:203
  1.8 0.7 %collective-permute-start = (bf16[2,1312,128]{2,1,0:T(8,128)(2,1)S(1)}, bf16[2,1312,128]{2,1,0:T(8,128)(2,1)S(1)}, u32[]{:S(2)}, u32[]{:S(2)}) collective-permute-start(bf16[2,1312,128]{2,1,0:T(8,128)(2,1)S(1)} %get-tuple-element.29), channel_id=1, source_target_pairs={{0,1},{1,0},{2,3},{3,2},{4,5},{5,4},{6,7},{7,6},{8,9},{9,8},{10,11... | collective-permute-start | bytes 2015240 | tf_op jit(solution)/shard_map/ppermute | solution.py:48
  2.6 0.1 collective-permute-start.1
  2.6 3.5 %collective-permute-start.2 = (bf16[1,1280,128]{2,1,0:T(8,128)(2,1)S(1)}, bf16[1,1280,128]{2,1,0:T(8,128)(2,1)S(1)}, u32[]{:S(2)}, u32[]{:S(2)}) collective-permute-start(bf16[1,1280,128]{2,1,0:T(8,128)(2,1)S(1)} %get-tuple-element.31), channel_id=1, source_target_pairs={{1,2},{2,1},{5,6},{6,5},{9,10},{10,9},{13,14},{14,13},{17,18},{18,... | collective-permute-start | bytes 983048 | tf_op jit(solution)/shard_map/ppermute | solution.py:48
  6.1 2.1 %collective-permute-start.3 = (bf16[1,1280,128]{2,1,0:T(8,128)(2,1)S(1)}, bf16[1,1280,128]{2,1,0:T(8,128)(2,1)S(1)}, u32[]{:S(2)}, u32[]{:S(2)}) collective-permute-start(bf16[1,1280,128]{2,1,0:T(8,128)(2,1)S(1)} %get-tuple-element.37), channel_id=1, source_target_pairs={{1,2},{2,1},{5,6},{6,5},{9,10},{10,9},{13,14},{14,13},{17,18},{18,... | collective-permute-start | bytes 983048 | tf_op jit(solution)/shard_map/ppermute | solution.py:48
  8.2 3.5 %collective-permute-start.4 = (bf16[2,1280,128]{2,1,0:T(8,128)(2,1)S(1)}, bf16[2,1280,128]{2,1,0:T(8,128)(2,1)S(1)}, u32[]{:S(2)}, u32[]{:S(2)}) collective-permute-start(bf16[2,1280,128]{2,1,0:T(8,128)(2,1)S(1)} %get-tuple-element.42), channel_id=1, source_target_pairs={{1,2},{2,1},{5,6},{6,5},{9,10},{10,9},{13,14},{14,13},{17,18},{18,... | collective-permute-start | bytes 1966088 | tf_op jit(solution)/shard_map/ppermute | solution.py:48
  11.7 0.0 collective-permute-done.2.far_ref
  11.7 0.0 collective-permute-done.core_ref
  11.7 1.3 %compress_near.1 = (bf16[2,256,384]{2,1,0:T(8,128)(2,1)S(1)}, bf16[3,256,128]{2,1,0:T(8,128)(2,1)S(1)}) custom-call(bf16[2,1024,384]{2,1,0:T(8,128)(2,1)S(1)} %get-tuple-element.28.s_ref, bf16[2,1312,128]{2,1,0:T(8,128)(2,1)S(1)} %collective-permute-done.core_ref, bf16[1,1280,128]{2,1,0:T(8,128)(2,1)S(1)} %collective-permute-done.2.far_ref, ...), custom_call_target="tpu_custom_call" | custom-call | tf_op jit(solution)/shard_map/compress_near/pallas_call | solution.py:298
  13.0 1.3 %collective-permute-start.5 = (bf16[2,256,384]{2,1,0:T(8,128)(2,1)S(1)}, bf16[2,256,384]{2,1,0:T(8,128)(2,1)S(1)}, u32[]{:S(2)}, u32[]{:S(2)}) collective-permute-start(bf16[2,256,384]{2,1,0:T(8,128)(2,1)S(1)} %get-tuple-element.43.near_ref), channel_id=1, source_target_pairs={{0,4},{4,0},{8,12},{12,8},{16,20},{20,16},{24,28},{28,24},{1,5},{5... | collective-permute-start | bytes 1179656 | tf_op jit(solution)/shard_map/ppermute | solution.py:48
  14.3 0.0 collective-permute-done.1.core_ref
  14.3 0.2 collective-permute-done.3.far_ref
  14.5 1.2 %compress_away.1.away_ref = bf16[2,256,384]{2,1,0:T(8,128)(2,1)S(1)} custom-call(bf16[2,1024,384]{2,1,0:T(8,128)(2,1)S(1)} %get-tuple-element.28.s_ref, bf16[2,1312,128]{2,1,0:T(8,128)(2,1)S(1)} %collective-permute-done.core_ref, bf16[1,1280,128]{2,1,0:T(8,128)(2,1)S(1)} %collective-permute-done.3.far_ref, bf16[1280,256]{1,0:T(8,128)(2,1)S(1)} %get-tuple-element.32.w_ref, ...), custom_call_target="tpu_custom_call" | custom-call | tf_op jit(solution)/shard_map/compress_away/pallas_call | solution.py:298
  15.7 3.3 %collective-permute-start.6 = (bf16[2,256,384]{2,1,0:T(8,128)(2,1)S(1)}, bf16[2,256,384]{2,1,0:T(8,128)(2,1)S(1)}, u32[]{:S(2)}, u32[]{:S(2)}) collective-permute-start(bf16[2,256,384]{2,1,0:T(8,128)(2,1)S(1)} %compress_away.1.away_ref), channel_id=1, source_target_pairs={{4,8},{8,4},{12,16},{16,12},{20,24},{24,20},{5,9},{9,5},{13,17},{1... | collective-permute-start | bytes 1179656 | tf_op jit(solution)/shard_map/ppermute | solution.py:48
  19.0 0.3 %azimuth_weights.1.a_ref = bf16[3,3,512,256]{3,2,1,0:T(8,128)(2,1)S(1)} custom-call(bf16[3,2,512]{2,1,0:T(2,128)(2,1)S(1)} %get-tuple-element.40.azimuth_ref), custom_call_target="tpu_custom_call" | custom-call | tf_op jit(solution)/shard_map/azimuth_weights/pallas_call | solution.py:114
  19.3 1.0 %focus_outer.1 = (f32[2,2,256,384]{3,2,1,0:T(8,128)S(1)}, f32[2,2,256,384]{3,2,1,0:T(8,128)S(1)}) custom-call(bf16[3,3,512,256]{3,2,1,0:T(8,128)(2,1)S(1)} %azimuth_weights.1.a_ref, bf16[2,256,384]{2,1,0:T(8,128)(2,1)S(1)} %get-tuple-element.43.near_ref, bf16[2,256,384]{2,1,0:T(8,128)(2,1)S(1)} %compress_away.1.away_ref), custom_call_target="tpu_custom_call" | custom-call | tf_op jit(solution)/shard_map/focus_outer/pallas_call | solution.py:351
  20.3 1.2 %collective-permute-done.4.far_ref = bf16[2,1280,128]{2,1,0:T(8,128)(2,1)S(1)} collective-permute-done((bf16[2,1280,128]{2,1,0:T(8,128)(2,1)S(1)}, bf16[2,1280,128]{2,1,0:T(8,128)(2,1)S(1)}, u32[]{:S(2)}, u32[]{:S(2)}) %collective-permute-start.4) | collective-permute-done | bytes 655392 | tf_op jit(solution)/shard_map/ppermute | solution.py:48
  21.6 2.1 %compress_mid.1.mid_ref = bf16[2,512,384]{2,1,0:T(8,128)(2,1)S(1)} custom-call(bf16[2,1024,384]{2,1,0:T(8,128)(2,1)S(1)} %get-tuple-element.28.s_ref, bf16[2,1296,128]{2,1,0:T(8,128)(2,1)S(1)} %collective-permute-done.1.core_ref, bf16[2,1280,128]{2,1,0:T(8,128)(2,1)S(1)} %collective-permute-done.4.far_ref, bf16[1280,256]{1,0:T(8,128)(2,1)S(1)} %get-tuple-element.32.w_ref, ...), custom_call_target="tpu_custom_call" | custom-call | tf_op jit(solution)/shard_map/compress_mid/pallas_call | solution.py:298
  23.7 2.0 %focus_mid.1 = (f32[2,1024,384]{2,1,0:T(8,128)}, f32[2,2,256,384]{3,2,1,0:T(8,128)S(1)}) custom-call(bf16[3,3,512,256]{3,2,1,0:T(8,128)(2,1)S(1)} %azimuth_weights.1.a_ref, bf16[2,512,384]{2,1,0:T(8,128)(2,1)S(1)} %compress_mid.1.mid_ref, f32[2,2,256,384]{3,2,1,0:T(8,128)S(1)} %get-tuple-element.47.part_ref, ...), custom_call_target="tpu_custom_call" | custom-call | tf_op jit(solution)/shard_map/focus_mid/pallas_call | solution.py:387
  25.7 1.8 %collective-permute-done.5.halo_ref = bf16[2,256,384]{2,1,0:T(8,128)(2,1)S(1)} collective-permute-done((bf16[2,256,384]{2,1,0:T(8,128)(2,1)S(1)}, bf16[2,256,384]{2,1,0:T(8,128)(2,1)S(1)}, u32[]{:S(2)}, u32[]{:S(2)}) %collective-permute-start.5) | collective-permute-done | bytes 393248 | tf_op jit(solution)/shard_map/ppermute | solution.py:48
  27.5 0.4 %near_end.1.near_ref = f32[2,256,384]{2,1,0:T(8,128)S(1)} custom-call(bf16[3,3,512,256]{3,2,1,0:T(8,128)(2,1)S(1)} %azimuth_weights.1.a_ref, f32[2,2,256,384]{3,2,1,0:T(8,128)S(1)} %get-tuple-element.49.part_ref, bf16[2,256,384]{2,1,0:T(8,128)(2,1)S(1)} %collective-permute-done.5.halo_ref), custom_call_target="tpu_custom_call" | custom-call | tf_op jit(solution)/shard_map/near_end/pallas_call | solution.py:413
  27.9 0.0 collective-permute-done.6.halo_ref
  27.9 1.2 %ends.1 = f32[2,1024,384]{2,1,0:T(8,128)} custom-call(bf16[3,3,512,256]{3,2,1,0:T(8,128)(2,1)S(1)} %azimuth_weights.1.a_ref, f32[2,2,256,384]{3,2,1,0:T(8,128)S(1)} %get-tuple-element.49.part_ref, f32[2,256,384]{2,1,0:T(8,128)S(1)} %near_end.1.near_ref, bf16[2,256,384]{2,1,0:T(8,128)(2,1)S(1)} %collective-permute-done.6.halo_ref, ...), custom_call_target="tpu_custom_call", output_to_operand_aliasing={{}: (4, {})} | custom-call | tf_op jit(solution)/shard_map/ends/pallas_call | solution.py:460
Async XLA Ops:
  1.8 9.9 %collective-permute-start = (bf16[2,1312,128]{2,1,0:T(8,128)(2,1)S(1)}, bf16[2,1312,128]{2,1,0:T(8,128)(2,1)S(1)}, u32[]{:S(2)}, u32[]{:S(2)}) collective-permute-start(bf16[2,1312,128]{2,1,0:T(8,128)(2,1)S(1)} %get-tuple-element.29), channel_id=1, source_target_pairs={{0,1},{1,0},{2,3},{3,2},{4,5},{5,4},{6,7},{7,6},{8,9},{9,8},{10,11... | collective-permute-start | bytes 2015240 | tf_op jit(solution)/shard_map/ppermute | solution.py:48
  2.6 11.7 %collective-permute-start.1 = (bf16[2,1296,128]{2,1,0:T(8,128)(2,1)S(1)}, bf16[2,1296,128]{2,1,0:T(8,128)(2,1)S(1)}, u32[]{:S(2)}, u32[]{:S(2)}) collective-permute-start(bf16[2,1296,128]{2,1,0:T(8,128)(2,1)S(1)} %get-tuple-element.30), channel_id=1, source_target_pairs={{0,1},{1,0},{2,3},{3,2},{4,5},{5,4},{6,7},{7,6},{8,9},{9,8},{10,11... | collective-permute-start | bytes 1990664 | tf_op jit(solution)/shard_map/ppermute | solution.py:48
  2.6 9.0 %collective-permute-start.2 = (bf16[1,1280,128]{2,1,0:T(8,128)(2,1)S(1)}, bf16[1,1280,128]{2,1,0:T(8,128)(2,1)S(1)}, u32[]{:S(2)}, u32[]{:S(2)}) collective-permute-start(bf16[1,1280,128]{2,1,0:T(8,128)(2,1)S(1)} %get-tuple-element.31), channel_id=1, source_target_pairs={{1,2},{2,1},{5,6},{6,5},{9,10},{10,9},{13,14},{14,13},{17,18},{18,... | collective-permute-start | bytes 983048 | tf_op jit(solution)/shard_map/ppermute | solution.py:48
  6.1 8.4 %collective-permute-start.3 = (bf16[1,1280,128]{2,1,0:T(8,128)(2,1)S(1)}, bf16[1,1280,128]{2,1,0:T(8,128)(2,1)S(1)}, u32[]{:S(2)}, u32[]{:S(2)}) collective-permute-start(bf16[1,1280,128]{2,1,0:T(8,128)(2,1)S(1)} %get-tuple-element.37), channel_id=1, source_target_pairs={{1,2},{2,1},{5,6},{6,5},{9,10},{10,9},{13,14},{14,13},{17,18},{18,... | collective-permute-start | bytes 983048 | tf_op jit(solution)/shard_map/ppermute | solution.py:48
  8.2 13.3 %collective-permute-start.4 = (bf16[2,1280,128]{2,1,0:T(8,128)(2,1)S(1)}, bf16[2,1280,128]{2,1,0:T(8,128)(2,1)S(1)}, u32[]{:S(2)}, u32[]{:S(2)}) collective-permute-start(bf16[2,1280,128]{2,1,0:T(8,128)(2,1)S(1)} %get-tuple-element.42), channel_id=1, source_target_pairs={{1,2},{2,1},{5,6},{6,5},{9,10},{10,9},{13,14},{14,13},{17,18},{18,... | collective-permute-start | bytes 1966088 | tf_op jit(solution)/shard_map/ppermute | solution.py:48
  13.0 14.5 %collective-permute-start.5 = (bf16[2,256,384]{2,1,0:T(8,128)(2,1)S(1)}, bf16[2,256,384]{2,1,0:T(8,128)(2,1)S(1)}, u32[]{:S(2)}, u32[]{:S(2)}) collective-permute-start(bf16[2,256,384]{2,1,0:T(8,128)(2,1)S(1)} %get-tuple-element.43.near_ref), channel_id=1, source_target_pairs={{0,4},{4,0},{8,12},{12,8},{16,20},{20,16},{24,28},{28,24},{1,5},{5... | collective-permute-start | bytes 1179656 | tf_op jit(solution)/shard_map/ppermute | solution.py:48
  15.7 12.2 %collective-permute-start.6 = (bf16[2,256,384]{2,1,0:T(8,128)(2,1)S(1)}, bf16[2,256,384]{2,1,0:T(8,128)(2,1)S(1)}, u32[]{:S(2)}, u32[]{:S(2)}) collective-permute-start(bf16[2,256,384]{2,1,0:T(8,128)(2,1)S(1)} %compress_away.1.away_ref), channel_id=1, source_target_pairs={{4,8},{8,4},{12,16},{16,12},{20,24},{24,20},{5,9},{9,5},{13,17},{1... | collective-permute-start | bytes 1179656 | tf_op jit(solution)/shard_map/ppermute | solution.py:48
